TPU v7x, 128 devices: a whole 4x4x4 slice. The times are simulated.
128 devices in a mesh: fsdp: 16 (over x, y), grp: 8 (over z, core).
Axes of the slice: x: 4, y: 4, z: 4, core: 2. Of those that a mesh axis runs over, the one named last changes fastest.
Arguments:
- hidden: bfloat16 [1024, 32768], P(('fsdp', 'grp')), may hold values from -6 to 6
- grad_out: bfloat16 [1024, 7424], P(('fsdp', 'grp')), may hold values from -0.0048828125 to 0.0048828125
- token_counts: int32 [128], P(('fsdp', 'grp')), may hold values from 1 to 8
- weight: bfloat16 [32768, 7424], P(('fsdp', 'grp')), may hold values from -0.0546875 to 0.0546875
- old_mask: int32 [256, 58], P(('fsdp', 'grp')), may hold values from 0 to 1, as said below
- drop_list: int32 [128, 7], P(('fsdp', 'grp')), may hold values from 0 to 115, as said below
- grow_list: int32 [128, 7], P(('fsdp', 'grp')), may hold values from 0 to 115, as said below
- inputs: bfloat16 [1024, 32768], P('grp', 'fsdp'), may hold values from -6 to 6
Outputs:
- outputs: bfloat16 [1024, 7424], P('grp', 'fsdp')
- new_mask: int32 [256, 58], P(('fsdp', 'grp'))
Inputs may be any that keep to these rules, and one draw needn't show every extreme that they name: `old_mask`: each owner keeps between 34 and 47 blocks, and some owner keeps exactly 47. `drop_list`: each owner's entries are distinct blocks that it keeps in old_mask. `grow_list`: each owner's entries are distinct blocks that it does not keep in old_mask.
All inputs are finite; a program needn't handle non-finite values.
Results may differ from a plain program's by a relative error of at most 0.02.
Values may be sent and summed in bfloat16 or wider, within the bound.
A program may use at most 128 MiB of HBM per device.

v0:
```python
import jax
import jax.numpy as jnp
from jax import lax
from jax.sharding import PartitionSpec as P


def shards(hidden, grad_out, token_counts, weight, old_mask, drop_list, grow_list, inputs):
    block_rows, col_blocks = old_mask.shape
    own_rows, model_width = weight.shape
    tile_side = own_rows // block_rows
    tok_dev = hidden.shape[0]
    fwd_rows = inputs.shape[0]
    n_fsdp = lax.axis_size("fsdp")
    n_grp = lax.axis_size("grp")
    owners = n_fsdp * n_grp
    blocks_dev = block_rows * col_blocks
    capacity = blocks_dev * 41 // 100
    valid_rows = jnp.arange(tok_dev) < token_counts[0]
    masked_grad = jnp.where(valid_rows[:, None], grad_out, jnp.zeros_like(grad_out))
    sections = hidden.reshape(tok_dev, owners, own_rows)
    arrived = lax.all_to_all(sections, ("fsdp", "grp"), split_axis=1, concat_axis=0, tiled=True)
    hidden_all = arrived.reshape(owners * tok_dev, own_rows)
    grad_own = lax.dot_general(
        hidden_all,
        lax.all_gather(masked_grad, ("fsdp", "grp"), axis=0, tiled=True),
        (((0,), (0,)), ((), ())),
        preferred_element_type=jnp.float32,
    )
    flat_old = old_mask.reshape(blocks_dev)
    slot_ids = jnp.arange(blocks_dev, dtype=jnp.int32)
    dropped = jnp.any(slot_ids[:, None] == drop_list[0][None, :], axis=1)
    grown = jnp.any(slot_ids[:, None] == grow_list[0][None, :], axis=1)
    flat_new = jnp.where(grown, 1, jnp.where(dropped, 0, flat_old))
    new_mask = flat_new.reshape(block_rows, col_blocks)

    def expand_mask(block_mask):
        widened = jnp.broadcast_to(
            block_mask[:, None, :, None], (block_rows, tile_side, col_blocks, tile_side)
        )
        return widened.reshape(own_rows, model_width).astype(jnp.float32)

    new_weight = (
        expand_mask(new_mask) * (expand_mask(old_mask) * weight.astype(jnp.float32) - grad_own)
    ).astype(jnp.bfloat16)
    kept_before = jnp.sum(
        jnp.where(slot_ids[None, :] < slot_ids[:, None], flat_new[None, :], 0), axis=1
    )
    slot_range = jnp.arange(capacity, dtype=jnp.int32)
    pick_table = (flat_new[None, :] == 1) & (kept_before[None, :] == slot_range[:, None])
    kept_order = jnp.sum(jnp.where(pick_table, slot_ids[None, :], 0), axis=1)
    tile_set = (
        new_weight.reshape(block_rows, tile_side, col_blocks, tile_side)
        .transpose(0, 2, 1, 3)
        .reshape(blocks_dev, tile_side, tile_side)
    )
    packed = jnp.einsum(
        "kp,pbc->kbc", pick_table.astype(jnp.bfloat16), tile_set, preferred_element_type=jnp.float32
    ).astype(jnp.bfloat16)
    xblocks = inputs.reshape(fwd_rows, n_grp * block_rows, tile_side)
    row_range = jnp.arange(n_grp * block_rows, dtype=jnp.int32)
    col_range = jnp.arange(col_blocks, dtype=jnp.int32)
    tiles_part = lax.all_gather(packed, "grp", axis=0, tiled=True)
    index_part = lax.all_gather(kept_order, "grp", axis=0, tiled=True)
    tile_count = index_part.shape[0]
    owner_part = jnp.arange(tile_count, dtype=jnp.int32) // capacity
    row_part = owner_part * block_rows + index_part // col_blocks
    col_part = index_part % col_blocks
    row_pick = (row_part[:, None] == row_range[None, :]).astype(jnp.bfloat16)
    chosen = jnp.einsum(
        "tjb,kj->tkb", xblocks, row_pick, preferred_element_type=jnp.float32
    ).astype(jnp.bfloat16)
    products = jnp.einsum("tkb,kbc->tkc", chosen, tiles_part, preferred_element_type=jnp.float32)
    upper_part = products.astype(jnp.bfloat16)
    lower_part = (products - upper_part.astype(jnp.float32)).astype(jnp.bfloat16)
    col_pick = (col_part[:, None] == col_range[None, :]).astype(jnp.bfloat16)
    placed = jnp.einsum("tkc,kn->tnc", upper_part, col_pick, preferred_element_type=jnp.float32)
    placed = placed + jnp.einsum(
        "tkc,kn->tnc", lower_part, col_pick, preferred_element_type=jnp.float32
    )
    summed = lax.psum_scatter(
        placed.astype(jnp.bfloat16)
        .astype(jnp.float32)
        .reshape(fwd_rows, model_width)
        .astype(jnp.bfloat16),
        "fsdp",
        scatter_dimension=1,
        tiled=True,
    )
    return (summed, new_mask)


def solution(mesh):
    placed = (
        P(("fsdp", "grp"), None),
        P(("fsdp", "grp"), None),
        P(("fsdp", "grp")),
        P(("fsdp", "grp"), None),
        P(("fsdp", "grp"), None),
        P(("fsdp", "grp"), None),
        P(("fsdp", "grp"), None),
        P("grp", "fsdp"),
    )
    return jax.shard_map(
        shards,
        mesh=mesh,
        in_specs=placed,
        out_specs=(P("grp", "fsdp"), P(("fsdp", "grp"), None)),
        check_vma=False,
    )
```

profile of v0, /device:TPU:1, one launch (start us, length us, event | category | flops | bytes accessed | tf_op | source)
XLA Modules:
  0.0 358.4 jit_solution(17349952375097177549)
XLA Ops:
  7.2 0.0 all-gather.3.cloned.1.call-start
  7.9 1.6 broadcast_select_fusion
  9.5 0.0 all-gather.3.cloned.1.call-update
  9.5 11.5 %all-to-all-start = ((bf16[8,128,256]{2,0,1:T(8,128)(2,1)}), bf16[8,128,256]{2,0,1:T(8,128)(2,1)S(1)}, u32[]{:S(2)}, u32[]{:S(2)}) async-start(bf16[8,128,256]{2,0,1:T(8,128)(2,1)} %bitcast.74), calls=%async_computation | async-start | bytes 1048576 | tf_op jit(solution)/shard_map/all_to_all | solution.py:21
  21.0 0.0 all-gather.5.cloned.1.call-start
  21.1 0.8 reshape.67
  21.8 0.8 fusion.27
  22.6 0.1 reduce_or.24
  22.7 0.1 reduce_or.25
  22.8 1.3 fusion.35
  24.1 0.1 copy.34
  24.2 0.1 copy.35
  24.3 6.2 %copy.36 = bf16[256,7424]{0,1:T(8,128)(2,1)} copy(bf16[256,7424]{1,0:T(8,128)(2,1)} %param.11) | data formatting | bytes 7602176 | tf_op args[3]
  30.5 0.1 select_reduce_fusion
  30.6 4.5 %all-to-all-done = bf16[8,128,256]{2,0,1:T(8,128)(2,1)S(1)} async-done(((bf16[8,128,256]{2,0,1:T(8,128)(2,1)}), bf16[8,128,256]{2,0,1:T(8,128)(2,1)S(1)}, u32[]{:S(2)}, u32[]{:S(2)}) %all-to-all-start) | async-done | bytes 524320 | tf_op jit(solution)/shard_map/all_to_all | solution.py:21
  35.1 58.1 %all-gather.3.cloned.1.call-done = bf16[1024,7424]{1,0:T(8,128)(2,1)} async-done(((bf16[8,7424]{1,0:T(8,128)(2,1)}), bf16[1024,7424]{1,0:T(8,128)(2,1)}) %all-gather.3.cloned.1.call-update) | async-done | bytes 15204368 | tf_op jit(solution)/shard_map/all_gather | solution.py:25
  93.2 0.0 copy-start.1
  93.2 5.1 %broadcast_in_dim.80 = f32[2,128,58,128]{1,0,3,2:T(2,128)} broadcast(f32[2,58]{0,1:T(8,128)S(1)} %copy.35), dimensions={0,2} | broadcast | bytes 7602640 | tf_op jit(solution)/shard_map/broadcast_in_dim | solution.py:37
  98.3 5.1 %broadcast_in_dim.79 = f32[2,128,58,128]{1,0,3,2:T(2,128)} broadcast(f32[2,58]{0,1:T(8,128)S(1)} %copy.34), dimensions={0,2} | broadcast | bytes 7602640 | tf_op jit(solution)/shard_map/broadcast_in_dim | solution.py:37
  103.4 0.0 copy-done.1
  103.4 16.1 %fusion.5 = bf16[256,7424]{0,1:T(8,128)(2,1)} fusion(bf16[1024,7424]{1,0:T(8,128)(2,1)} %all-gather.3.cloned.1.call-done, f32[928,8,2,128]{3,2,1,0:T(2,128)} %bitcast.70, f32[928,8,2,128]{3,2,1,0:T(2,128)} %bitcast.71, bf16[256,7424]{0,1:T(8,128)(2,1)S(1)} %copy-done.1, bf16[8,128,256]{2,0,1:T(8,128)(2,1)S(1)} %all-to-all-done), kind=kOutput, calls=%fused_computation.9 | convolution fusion | flops 3901816832 | bytes 38535168 | tf_op jit(solution)/shard_map/dot_general | solution.py:23
  119.5 8.1 %reshape.70 = bf16[2,128,58,128]{1,0,3,2:T(2,128)(2,1)} reshape(bf16[256,7424]{0,1:T(8,128)(2,1)} %fusion.5) | data formatting | bytes 7602176 | tf_op jit(solution)/shard_map/reshape | solution.py:52
  127.6 0.0 copy-start.2
  127.6 0.0 copy-start.3
  127.6 10.5 %copy.37 = bf16[2,128,58,128]{3,1,2,0:T(8,128)(2,1)} copy(bf16[2,128,58,128]{1,0,3,2:T(2,128)(2,1)} %reshape.70) | data formatting | bytes 7602176 | tf_op jit(solution)/shard_map/reshape | solution.py:52
  138.1 4.8 %fusion.8 = bf16[47,128,128]{2,0,1:T(8,128)(2,1)S(1)} fusion(bf16[116,128,128]{2,1,0:T(8,128)(2,1)} %bitcast.69, s32[116]{0:T(128)S(1)} %select_reduce_fusion, pred[116]{0:T(512)(128)(4,1)S(1)} %get-tuple-element.4), kind=kOutput, calls=%fused_computation.14 | convolution fusion | flops 179432096 | bytes 5341764 | tf_op jit(solution)/shard_map/kp,pbc->kbc/dot_general | solution.py:56
  142.9 1.6 copy.39
  144.5 0.0 all-gather.5.cloned.1.call-update
  144.5 0.0 reduce-scatter.4.cloned.1.call-start
  144.5 0.0 copy-done.2
  144.6 0.1 copy.48
  144.7 0.0 copy-done.3
  144.7 0.6 dynamic-slice
  145.9 0.1 select_reduce_fusion.1
  146.1 0.2 dynamic-update-slice
  146.3 7.2 %all-reduce = s32[376]{0:T(512)S(1)} all-reduce(s32[376]{0:T(512)S(1)} %dynamic-update-slice), channel_id=1, replica_groups=mesh['fsdp'=16,'grp'=8] {'grp'}, use_global_device_ids=true, to_apply=%add | all-reduce | flops 376 | bytes 3008
  153.5 6.7 %convert_bitcast_fusion = bf16[128,376,128]{2,1,0:T(8,128)(2,1)} fusion(bf16[128,16,128]{2,1,0:T(8,128)(2,1)S(1)} %bitcast.73, s32[376]{0:T(512)S(1)} %get-tuple-element.9), kind=kOutput, calls=%fused_computation.5 | convolution fusion | flops 203298688 | bytes 12846560 | tf_op jit(solution)/shard_map/tjb,kj->tkb/dot_general | solution.py:69
  160.2 50.4 %all-gather.5.cloned.1.call-done = bf16[376,128,128]{2,1,0:T(8,128)(2,1)} async-done(((bf16[47,128,128]{2,1,0:T(8,128)(2,1)}), bf16[376,128,128]{2,1,0:T(8,128)(2,1)}) %all-gather.5.cloned.1.call-update) | async-done | bytes 12320784 | tf_op jit(solution)/shard_map/all_gather | solution.py:62
  210.6 22.6 %fusion = (bf16[128,376,128]{0,2,1:T(8,128)(2,1)}, bf16[128,376,128]{0,2,1:T(8,128)(2,1)}) fusion(bf16[376,128,128]{2,1,0:T(8,128)(2,1)} %all-gather.5.cloned.1.call-done, bf16[128,376,128]{2,1,0:T(8,128)(2,1)} %convert_bitcast_fusion), kind=kOutput, calls=%fused_computation.2 | convolution fusion | flops 1601699840 | bytes 49283072 | tf_op jit(solution)/shard_map/tkb,kbc->tkc/dot_general | solution.py:72
  233.2 16.5 %copy.43 = bf16[128,376,128]{2,1,0:T(8,128)(2,1)} copy(bf16[128,376,128]{0,2,1:T(8,128)(2,1)} %get-tuple-element.2) | data formatting | bytes 24641536 | tf_op jit(solution)/shard_map/convert_element_type | solution.py:74
  249.7 16.7 %copy.42 = bf16[128,376,128]{2,1,0:T(8,128)(2,1)} copy(bf16[128,376,128]{0,2,1:T(8,128)(2,1)} %get-tuple-element.3) | data formatting | bytes 24641536 | tf_op jit(solution)/shard_map/convert_element_type | solution.py:73
  266.4 0.0 copy-start
  266.4 7.0 %fusion.15 = f32[58,128,128]{2,0,1:T(8,128)S(1)} fusion(bf16[128,376,128]{2,1,0:T(8,128)(2,1)} %copy.42, s32[376]{0:T(512)S(1)} %get-tuple-element.8), kind=kOutput, calls=%fused_computation.20 | convolution fusion | flops 714626368 | bytes 16123360 | tf_op jit(solution)/shard_map/tkc,kn->tnc/dot_general | solution.py:76
  273.4 1.0 copy-done
  274.4 2.3 fusion.11
  276.7 2.8 copy.44
  279.6 0.0 reduce-scatter.4.cloned.1.call-update
  279.6 72.3 %reduce-scatter.4.cloned.1.call-done = bf16[128,464]{0,1:T(8,128)(2,1)} async-done(((bf16[128,7424]{0,1:T(8,128)(2,1)}), bf16[128,464]{0,1:T(8,128)(2,1)}) %reduce-scatter.4.cloned.1.call-update) | async-done | bytes 118800
  (4 shorter events, 0.0 us)
Async XLA Ops:
  7.2 86.1 %all-gather.3.cloned.1.call-start = ((), (), s32[]{:S(2)}) async-start(), calls=%async_computation.2 | async-start | bytes 15323136 | tf_op jit(solution)/shard_map/all_gather | solution.py:25
  9.5 25.6 %all-to-all-start = ((bf16[8,128,256]{2,0,1:T(8,128)(2,1)}), bf16[8,128,256]{2,0,1:T(8,128)(2,1)S(1)}, u32[]{:S(2)}, u32[]{:S(2)}) async-start(bf16[8,128,256]{2,0,1:T(8,128)(2,1)} %bitcast.74), calls=%async_computation | async-start | bytes 1048576 | tf_op jit(solution)/shard_map/all_to_all | solution.py:21
  21.0 189.6 %all-gather.5.cloned.1.call-start = ((), (), s32[]{:S(2)}) async-start(), calls=%async_computation.3 | async-start | bytes 13860864 | tf_op jit(solution)/shard_map/all_gather | solution.py:62
  93.2 10.2 %copy-start.1 = (bf16[256,7424]{0,1:T(8,128)(2,1)S(1)}, bf16[256,7424]{0,1:T(8,128)(2,1)}, u32[]{:S(2)}) copy-start(bf16[256,7424]{0,1:T(8,128)(2,1)} %copy.36) | copy-start | bytes 11403268
  127.6 16.9 %copy-start.2 = (bf16[128,2048]{1,0:T(8,128)(2,1)S(1)}, bf16[128,2048]{1,0:T(8,128)(2,1)}, u32[]{:S(2)}) copy-start(bf16[128,2048]{1,0:T(8,128)(2,1)} %param.15) | copy-start | bytes 1572868
  127.6 17.1 %copy-start.3 = (u32[128]{0:T(128)S(1)}, u32[128]{0:T(128)}, u32[]{:S(2)}) copy-start(u32[128]{0:T(128)} %constant.43) | copy-start | bytes 1540
  144.5 207.4 %reduce-scatter.4.cloned.1.call-start = ((), (), s32[]{:S(2)}) async-start(), calls=%async_computation.4 | async-start | bytes 2019328
  266.4 8.0 %copy-start = (bf16[128,376,128]{2,1,0:T(8,128)(2,1)S(1)}, bf16[128,376,128]{2,1,0:T(8,128)(2,1)}, u32[]{:S(2)}) copy-start(bf16[128,376,128]{2,1,0:T(8,128)(2,1)} %copy.43) | copy-start | bytes 36962308
Sparse Core Ops, SparseCore 0:
  11.5 81.6 all-gather.2
  144.6 65.9 all-gather.4
  279.7 72.1 reduce-scatter.3
where the time goes:
time: 361 us; the launch traced here: 358 us
  waiting for transfers between devices  185 us (51%)
  local copies, waits for them, and re-layouts  75.6 us (21%)
  matrix products  59.4 us (16%)
  between operations  15.1 us (4%)
  starting transfers between devices  11.6 us (3%)
  blocking collectives  7.23 us (2%)
  other arithmetic  3.96 us (1%)
    unnamed x4, waiting for transfers between devices  72.4 us
    all_gather x1, waiting for transfers between devices, shards(): lax.all_gather(masked_grad, ('fsdp', 'grp'), axis=0, tiled=True)  58.1 us
    all_gather x1, waiting for transfers between devices, shards(): tiles_part = lax.all_gather(packed, 'grp', axis=0, tiled=True)  50.4 us
    dot_general x1, matrix products, shards(): jnp.einsum('tkb,kbc->tkc', chosen, tiles_part, preferred_element_type=jnp...  22.6 us
    reshape x2, local copies, waits for them, and re-layouts, shards(): new_weight.reshape(block_rows, tile_side, col_blocks, tile_side)  18.6 us
    convert_element_type x1, local copies, waits for them, and re-layouts, shards(): upper_part = products.astype(jnp.bfloat16)  16.7 us
    convert_element_type x1, local copies, waits for them, and re-layouts, shards(): (products - upper_part.astype(jnp.float32)).astype(jnp.bfloat16)  16.5 us
    dot_general x1, matrix products, shards(): lax.dot_general(hidden_all, lax.all_gather(masked_grad, ('fsdp', 'grp'),...  16.1 us
  transfers between devices with their start and end apart: 4, of which 4 were waited for; matrix products, arithmetic and copies ran while one was open for 5% of the time, Pallas kernels for 0%

commit v1 on v0

v1 whole, which is shorter than its diff:
```python
import jax
import jax.numpy as jnp
from jax import lax
from jax.experimental import pallas as pl
from jax.experimental.pallas import tpu as pltpu
from jax.sharding import PartitionSpec as P

MESH = pl.DeviceIdType.MESH
BF = jnp.bfloat16
F32 = jnp.float32

RING = 4
ROWS = 16
BLK = 128
HALF = 3712
OWN = 256
CHUNK = 464
PAD = 512

PARTS = ((0, 1280, 640), (1280, 1280, 640), (2560, 1152, 640))
GATHER = (("x", "y", "z"), ("y", "z", "x"), ("z", "x", "y"))
SCATTER = (("x", "y", "z"), ("y", "z", "x"), ("z", "x", "y"))
GDIMS = ("x", "y", "z")
SDIMS = ("z", "x", "y")


def pick(dims, fixed):
    return tuple(fixed[d] if d in fixed else slice(None) for d in dims)


def kernel(
    count_ref, drop_ref, grow_ref, old_ref, grad_ref, hid_ref, inp_ref, w_ref,
    out_ref, mask_ref,
    gm, gpar, g, h, ht, acc, w, xin, s, m, expand, ra1, rb1, ra2, rb2, ra3, rb3, fin, stage, land,
    g_send, g_recv, s_send, s_recv, e_send, e_recv, f_send, f_recv, loc,
):
    fsdp = lax.axis_index("fsdp")
    grp = lax.axis_index("grp")
    me = {"x": fsdp // RING, "y": fsdp % RING, "z": grp // 2}
    core = grp % 2

    def dev(x, y, z, c):
        return (x * RING + y, z * 2 + c)

    def near(axis, step):
        at = dict(me)
        at[axis] = (at[axis] + step) % RING
        return dev(at["x"], at["y"], at["z"], core)

    partner = dev(me["x"], me["y"], me["z"], 1 - core)

    mine = pl.ds(pl.multiple_of(core * HALF, BLK), HALF)
    other = pl.ds(pl.multiple_of((1 - core) * HALF, BLK), HALF)
    local = [
        pltpu.make_async_copy(w_ref.at[:, mine], w.at[pl.ds(0, OWN), :], loc.at[0]),
        pltpu.make_async_copy(hid_ref, h.at[0], loc.at[1]),
        pltpu.make_async_copy(inp_ref, xin.at[0], loc.at[2]),
    ]
    for c in local:
        c.start()

    bar = pltpu.get_barrier_semaphore()
    for axis in ("x", "y", "z"):
        for step in (1, -1):
            pl.semaphore_signal(bar, inc=1, device_id=near(axis, step), device_id_type=MESH)
    pl.semaphore_signal(bar, inc=1, device_id=partner, device_id_type=MESH)
    last_core = me["x"] // 2
    self_in = last_core == core
    own_k = (me["x"] % 2) * RING + me["y"]

    def last_dev(k):
        return dev(2 * core + k // RING, k % RING, me["z"], last_core)

    def is_self(k):
        return jnp.logical_and(self_in, own_k == k)

    for k in range(8):
        @pl.when(jnp.logical_not(is_self(k)))
        def _():
            pl.semaphore_signal(bar, inc=1, device_id=last_dev(k), device_id_type=MESH)

    rows = lax.broadcasted_iota(jnp.int32, grad_ref.shape, 0)
    gm[...] = jnp.where(rows < count_ref[0], grad_ref[...].astype(F32), 0.0).astype(BF)

    old = old_ref[...]
    ids = lax.broadcasted_iota(jnp.int32, old.shape, 0) * old.shape[1] + lax.broadcasted_iota(
        jnp.int32, old.shape, 1
    )
    new = old
    for k in range(drop_ref.shape[1]):
        new = jnp.where(ids == drop_ref[0, k], 0, new)
    for k in range(grow_ref.shape[1]):
        new = jnp.where(ids == grow_ref[0, k], 1, new)
    mask_ref[...] = new
    m[0] = jnp.zeros_like(m[0])
    m[0, 0:2, 0 : old.shape[1]] = new.astype(F32)
    m[0, 2:4, 0 : old.shape[1]] = (new * old).astype(F32)

    pl.semaphore_wait(bar, jnp.where(self_in, 14, 15))

    def remote(src, dst, sends, recvs, i, to):
        return pltpu.make_async_remote_copy(
            src_ref=src, dst_ref=dst, send_sem=sends.at[i], recv_sem=recvs.at[i],
            device_id=to, device_id_type=MESH,
        )

    swap = [
        remote(gm.at[:, other], gpar, e_send, e_recv, 0, partner),
        remote(m.at[0], m.at[1], e_send, e_recv, 1, partner),
        remote(hid_ref, h.at[1], e_send, e_recv, 2, partner),
        remote(w_ref.at[:, other], w.at[pl.ds(OWN, OWN), :], e_send, e_recv, 3, partner),
        remote(inp_ref, xin.at[1], e_send, e_recv, 4, partner),
    ]
    for c in swap:
        c.start()

    swap[0].wait_recv()
    a, b = gm[:, mine], gpar[...]
    first = core == 0
    g[me["x"], me["y"], me["z"]] = jnp.concatenate(
        [jnp.where(first, a, b), jnp.where(first, b, a)], axis=0
    )

    def gather_copy(p, q, j):
        off, width, half = PARTS[p]
        axis = GATHER[p][q]
        fixed = {d: me[d] for d in GATHER[p][q:]}
        if j == 0 or j == 1:
            cols = pl.ds(off, width)
            to = near(axis, 1 if j == 0 else -1)
        elif j == 2:
            fixed[axis] = (me[axis] - 1) % RING
            cols = pl.ds(off, half)
            to = near(axis, 1)
        else:
            fixed[axis] = (me[axis] + 1) % RING
            cols = pl.ds(off + half, width - half)
            to = near(axis, -1)
        ref = g.at[(*pick(GDIMS, fixed), slice(None), cols)]
        return remote(ref, ref, g_send, g_recv, (p * 3 + q) * 4 + j, to)

    gc = {(p, q, j): gather_copy(p, q, j) for p in range(3) for q in range(3) for j in range(4)}

    def tiles(p, body):
        off, width, _ = PARTS[p]
        whole = width // 256

        def step(t, carry):
            body(pl.multiple_of(off + t * 256, BLK), 256)
            return carry

        lax.fori_loop(0, whole, step, 0)
        if width % 256:
            body(off + whole * 256, width % 256)

    def grad_chunk(p, at, start):
        lhs = ht[p, at]
        sel = pick(GDIMS, {GATHER[p][2]: at})

        def body(o, n):
            rhs = g[(*sel, slice(None), pl.ds(o, n))].reshape(256, n)
            part = jnp.dot(lhs, rhs, preferred_element_type=F32)
            if start:
                acc[:, pl.ds(o, n)] = part
            else:
                acc[:, pl.ds(o, n)] += part

        tiles(p, body)

    for p in range(3):
        gc[p, 0, 0].start()
        gc[p, 0, 1].start()

    swap[1].wait_recv()

    def spread(t, carry):
        o = pl.multiple_of(t * BLK, BLK)
        block = lax.broadcasted_iota(jnp.int32, (BLK, BLK), 0) == core * (HALF // BLK) + t
        for i in range(2):
            expand[i, :, pl.ds(o, BLK)] = jnp.dot(
                m[i], block.astype(F32), preferred_element_type=F32
            )
        return carry

    def turn(i, carry):
        for p in range(3):
            sel = pick(GDIMS, {GATHER[p][2]: i})
            for side in range(2):
                part = h[(side, *sel)].reshape(256, OWN)
                ht[p, i, pl.ds(side * OWN, OWN), :] = part.T
        return carry

    for q in range(3):
        for p in range(3):
            gc[p, q, 0].wait_recv()
            gc[p, q, 2].start()
            gc[p, q, 1].wait_recv()
            gc[p, q, 3].start()
            if q == 2:
                axis = GATHER[p][2]
                grad_chunk(p, (me[axis] + 3) % RING, False)
                grad_chunk(p, (me[axis] + 1) % RING, False)
        if q == 0:
            lax.fori_loop(0, HALF // BLK, spread, 0)
        if q < 2:
            for p in range(3):
                gc[p, q, 2].wait_recv()
                gc[p, q, 3].wait_recv()
                gc[p, q + 1, 0].start()
                gc[p, q + 1, 1].start()
        if q == 0:
            local[1].wait()
            swap[2].wait_recv()
            lax.fori_loop(0, RING, turn, 0)
        if q == 1:
            for p in range(3):
                grad_chunk(p, me[GATHER[p][2]], True)
            local[0].wait()
            swap[3].wait_recv()
            local[2].wait()
            swap[4].wait_recv()

    ras, rbs = (ra1, ra2, ra3), (rb1, rb2, rb3)

    def scatter_copy(p, q, j):
        off, width, half = PARTS[p]
        axis = SCATTER[p][q]
        fixed = {d: me[d] for d in SCATTER[p][:q]}
        lo, hi = pl.ds(off, half), pl.ds(off + half, width - half)
        step = 1 if j % 2 == 0 else -1
        if j < 2:
            fixed[axis] = (me[axis] + 2) % RING
            cols = lo if j == 0 else hi
            into = ras[q]
        else:
            fixed[axis] = (me[axis] + step) % RING
            cols = (hi, lo, lo, hi)[j - 2]
            into = rbs[q].at[j % 2]
        src = s.at[(*pick(SDIMS, fixed), slice(None), cols)]
        dst = into.at[(*([slice(None)] * (3 - q)), cols)]
        return remote(src, dst, s_send, s_recv, (p * 3 + q) * 6 + j, near(axis, step))

    sc = {(p, q, j): scatter_copy(p, q, j) for p in range(3) for q in range(3) for j in range(6)}

    def out_chunk(p, at):
        sel = pick(SDIMS, {SCATTER[p][0]: at})
        left = xin[(0, *sel)].reshape(256, OWN)
        right = xin[(1, *sel)].reshape(256, OWN)

        def body(o, n):
            cols = pl.ds(o, n)
            part = jnp.dot(left, w[0:OWN, cols], preferred_element_type=F32)
            part = part + jnp.dot(right, w[OWN : 2 * OWN, cols], preferred_element_type=F32)
            s[(*sel, slice(None), cols)] = part.astype(BF).reshape(RING, RING, ROWS, n)

        tiles(p, body)

    def update(p):
        def body(o, n):
            cols = pl.ds(o, n)
            for r in range(4):
                side, row = r // 2, r % 2
                keep = expand[side, row : row + 1, cols]
                both = expand[side, row + 2 : row + 3, cols]
                span = pl.ds(r * BLK, BLK)
                w[span, cols] = (both * w[span, cols].astype(F32) - keep * acc[span, cols]).astype(BF)

        tiles(p, body)

    for p in range(3):
        gc[p, 2, 2].wait_recv()
        gc[p, 2, 3].wait_recv()
        axis = SCATTER[p][0]
        grad_chunk(p, (me[GATHER[p][2]] + 2) % RING, False)
        update(p)
        out_chunk(p, (me[axis] + 2) % RING)
        sc[p, 0, 0].start()
        sc[p, 0, 1].start()
    for p in range(3):
        axis = SCATTER[p][0]
        out_chunk(p, (me[axis] + 1) % RING)
        sc[p, 0, 2].start()
        out_chunk(p, (me[axis] + 3) % RING)
        sc[p, 0, 3].start()

    def add_into(p, q, v, cols, froms):
        fixed = {d: me[d] for d in SCATTER[p][:q]}
        fixed[SCATTER[p][q]] = v
        free = [d for d in SDIMS if d not in fixed]

        def one(lead):
            idx = dict(fixed)
            if free:
                idx[free[0]] = lead
            at = (*pick(SDIMS, idx), slice(None), cols)
            there = ((lead,) if free else ()) + (slice(None),) * (len(free) - 1 if free else 0)
            total = s[at].astype(F32)
            for ref, pre in froms:
                total = total + ref[(*pre, *there, slice(None), cols)].astype(F32)
            return at, total

        if not free:
            return one(None)

        def step(i, carry):
            at, total = one(i)
            s[at] = total.astype(BF)
            return carry

        lax.fori_loop(0, RING, step, 0)
        return None

    def store(done):
        if done is not None:
            s[done[0]] = done[1].astype(BF)

    for q in range(3):
        for p in range(3):
            off, width, half = PARTS[p]
            lo, hi = pl.ds(off, half), pl.ds(off + half, width - half)
            axis = SCATTER[p][q]
            sc[p, q, 0].wait_recv()
            store(add_into(p, q, (me[axis] + 1) % RING, lo, [(ras[q], ())]))
            sc[p, q, 4].start()
            sc[p, q, 1].wait_recv()
            store(add_into(p, q, (me[axis] + 3) % RING, hi, [(ras[q], ())]))
            sc[p, q, 5].start()
        for p in range(3):
            off, width, half = PARTS[p]
            axis = SCATTER[p][q]
            if q == 0:
                out_chunk(p, me[axis])
        for p in range(3):
            off, width, half = PARTS[p]
            axis = SCATTER[p][q]
            for j in (2, 3, 4, 5):
                sc[p, q, j].wait_recv()
            done = add_into(
                p, q, me[axis], pl.ds(off, width), [(rbs[q], (0,)), (rbs[q], (1,))]
            )
            if q < 2:
                for j in range(4):
                    sc[p, q + 1, j].start()
            else:
                fin[:, pl.ds(off, width)] = done[1]

    fin[:, pl.ds(HALF, BLK)] = jnp.zeros((ROWS, BLK), F32)
    slot = fsdp % 8
    ends = []
    for k in range(8):
        base, shift = CHUNK * k // BLK * BLK, CHUNK * k % BLK
        piece = fin[:, pl.ds(base, PAD + BLK)]
        if shift:
            piece = pltpu.roll(piece, PAD + BLK - shift, 1)
        stage[k] = piece[:, :PAD].astype(BF)
        far = pltpu.make_async_remote_copy(
            src_ref=stage.at[k], dst_ref=land.at[slot], send_sem=f_send.at[k],
            recv_sem=f_recv.at[slot], device_id=last_dev(k), device_id_type=MESH,
        )
        near_copy = pltpu.make_async_copy(stage.at[k], land.at[slot], f_recv.at[slot])

        @pl.when(jnp.logical_not(is_self(k)))
        def _():
            far.start()

        @pl.when(is_self(k))
        def _():
            near_copy.start()

        ends.append(far)
    for k in range(8):
        pltpu.make_async_copy(stage.at[k], land.at[k], f_recv.at[k]).wait()
        out_ref[pl.ds(k * ROWS, ROWS), :] = land[k][:, :CHUNK]

    for k in range(8):
        @pl.when(jnp.logical_not(is_self(k)))
        def _():
            ends[k].wait_send()
    for c in swap:
        c.wait_send()
    for c in gc.values():
        c.wait_send()
    for c in sc.values():
        c.wait_send()


def shards(hidden, grad_out, token_counts, weight, old_mask, drop_list, grow_list, inputs):
    sections = hidden.reshape(8, 128, OWN)
    hid = lax.all_to_all(sections, ("fsdp", "grp"), split_axis=1, concat_axis=0, tiled=True)
    hid = hid.reshape(RING, RING, RING, ROWS, OWN)
    inp = lax.all_to_all(
        inputs.reshape(128, 8, OWN), "grp", split_axis=1, concat_axis=0, tiled=True
    ).reshape(RING, RING, RING, ROWS, OWN)
    vmem = pl.BlockSpec(memory_space=pltpu.VMEM)
    smem = pl.BlockSpec(memory_space=pltpu.SMEM)
    hbm = pl.BlockSpec(memory_space=pl.ANY)
    dma = pltpu.SemaphoreType.DMA
    cube = (RING, RING, RING, ROWS)
    out, mask = pl.pallas_call(
        kernel,
        out_shape=(
            jax.ShapeDtypeStruct((128, CHUNK), BF),
            jax.ShapeDtypeStruct(old_mask.shape, jnp.int32),
        ),
        in_specs=[smem, smem, smem, vmem, vmem, hbm, hbm, hbm],
        out_specs=(vmem, vmem),
        scratch_shapes=[
            pltpu.VMEM((8, 2 * HALF), BF),
            pltpu.VMEM((8, HALF), BF),
            pltpu.VMEM((*cube, HALF), BF),
            pltpu.VMEM((2, *cube, OWN), BF),
            pltpu.VMEM((3, RING, 2 * OWN, 256), BF),
            pltpu.VMEM((2 * OWN, HALF), F32),
            pltpu.VMEM((2 * OWN, HALF), BF),
            pltpu.VMEM((2, *cube, OWN), BF),
            pltpu.VMEM((*cube, HALF), BF),
            pltpu.VMEM((2, 8, BLK), F32),
            pltpu.VMEM((2, 8, HALF), F32),
            pltpu.VMEM((RING, RING, ROWS, HALF), BF),
            pltpu.VMEM((2, RING, RING, ROWS, HALF), BF),
            pltpu.VMEM((RING, ROWS, HALF), BF),
            pltpu.VMEM((2, RING, ROWS, HALF), BF),
            pltpu.VMEM((ROWS, HALF), BF),
            pltpu.VMEM((2, ROWS, HALF), BF),
            pltpu.VMEM((ROWS, HALF + BLK), F32),
            pltpu.VMEM((8, ROWS, PAD), BF),
            pltpu.VMEM((8, ROWS, PAD), BF),
            dma((36,)), dma((36,)), dma((54,)), dma((54,)), dma((5,)), dma((5,)),
            dma((8,)), dma((8,)), dma((3,)),
        ],
        compiler_params=pltpu.CompilerParams(
            collective_id=0, has_side_effects=True, vmem_limit_bytes=60 * 2**20
        ),
        cost_estimate=pl.CostEstimate(flops=8 * 10**9, bytes_accessed=10**7, transcendentals=0),
    )(token_counts, drop_list, grow_list, old_mask, grad_out, hid, inp, weight)
    return (out, mask)


def solution(mesh):
    split = P(("fsdp", "grp"), None)
    return jax.shard_map(
        shards,
        mesh=mesh,
        in_specs=(split, split, P(("fsdp", "grp")), split, split, split, split, P("grp", "fsdp")),
        out_specs=(P("grp", "fsdp"), split),
        check_vma=False,
    )
```

time: 361 us -> 141 us (0.39)
  waiting for transfers between devices: 185 us -> 13 us
  Pallas kernels: 0 us -> 97.8 us
  local copies, waits for them, and re-layouts: 75.6 us -> 4.79 us
  matrix products: 59.4 us -> 0 us
  between operations: 15.1 us -> 1.3 us
  blocking collectives: 7.23 us -> 16.1 us
  other arithmetic: 3.96 us -> 0 us
    all_gather x2 -> x0, waiting for transfers between devices: 109 us -> none  [the longest x1 58.1 us: shards(): lax.all_gather(masked_grad, ('fsdp', 'grp'), axis=0, tiled=True)]
    pallas_call x0 -> x1, Pallas kernels: none -> 97.8 us  [shards(): pl.pallas_call(kernel, out_shape=(jax.ShapeDtypeStruct((128, CHUNK), BF),...]
    unnamed x4 -> x0, waiting for transfers between devices: 72.4 us -> none
    dot_general x6 -> x0, matrix products: 59.4 us -> none  [the longest x1 22.6 us: shards(): jnp.einsum('tkb,kbc->tkc', chosen, tiles_part, preferred_element_type=jnp...]
    convert_element_type x6 -> x0, local copies, waits for them, and re-layouts: 37.8 us -> none  [the longest x1 16.7 us: shards(): upper_part = products.astype(jnp.bfloat16)]
    reshape x3 -> x1, local copies, waits for them, and re-layouts: 19.4 us -> 1.08 us  [shards(): inputs.reshape(128, 8, OWN)]
    all_to_all x0 -> x1, blocking collectives: none -> 16.1 us  [shards(): lax.all_to_all(inputs.reshape(128, 8, OWN), 'grp', split_axis=1, concat_a...]
    broadcast_in_dim x2 -> x0, local copies, waits for them, and re-layouts: 10.2 us -> none  [expand_mask(): jnp.broadcast_to(block_mask[:, None, :, None], (block_rows, tile_side, co...]
  transfers between devices with their start and end apart: 4 -> 1, of which waited for: 4 -> 1; matrix products, arithmetic and copies ran while one was open for 5% -> 0% of each run, Pallas kernels for 0% -> 0%
where the time goes in v1:
time: 141 us
  Pallas kernels  97.8 us (69%)
  blocking collectives  16.1 us (11%)
  waiting for transfers between devices  13 us (9%)
  starting transfers between devices  8.16 us (6%)
  local copies, waits for them, and re-layouts  4.79 us (3%)
    pallas_call x1, Pallas kernels, shards(): pl.pallas_call(kernel, out_shape=(jax.ShapeDtypeStruct((128, CHUNK), BF),...  97.8 us
    all_to_all x1, blocking collectives, shards(): lax.all_to_all(inputs.reshape(128, 8, OWN), 'grp', split_axis=1, concat_a...  16.1 us
    all_to_all x1, waiting for transfers between devices, shards(): lax.all_to_all(sections, ('fsdp', 'grp'), split_axis=1, concat_axis=0, ti...  13 us
    all_to_all x1, starting transfers between devices, shards(): lax.all_to_all(sections, ('fsdp', 'grp'), split_axis=1, concat_axis=0, ti...  8.16 us
  transfers between devices with their start and end apart: 1, of which 1 were waited for; matrix products, arithmetic and copies ran while one was open for 0% of the time, Pallas kernels for 0%

profile of v1, /device:TPU:1, one launch (start us, length us, event | category | flops | bytes accessed | tf_op | source)
XLA Modules:
  0.0 141.2 jit_solution(1705025576343458698)
XLA Ops:
  0.6 1.1 copy.14
  1.7 16.1 %all_to_all.30 = bf16[128,8,256]{2,0,1:T(8,128)(2,1)} all-to-all(bf16[128,8,256]{2,0,1:T(8,128)(2,1)S(1)} %bitcast.15), channel_id=1, replica_groups=mesh['fsdp'=16,'grp'=8] {'grp'}, dimensions={1} | all-to-all | bytes 1048576 | tf_op jit(solution)/shard_map/all_to_all | solution.py:391
  17.8 8.2 %all-to-all-start = ((bf16[8,128,256]{2,0,1:T(8,128)(2,1)}), bf16[8,128,256]{2,0,1:T(8,128)(2,1)S(1)}, u32[]{:S(2)}, u32[]{:S(2)}) async-start(bf16[8,128,256]{2,0,1:T(8,128)(2,1)} %bitcast.17), calls=%async_computation | async-start | bytes 1048576 | tf_op jit(solution)/shard_map/all_to_all | solution.py:389
  26.6 13.0 %all-to-all-done = bf16[8,128,256]{2,0,1:T(8,128)(2,1)S(1)} async-done(((bf16[8,128,256]{2,0,1:T(8,128)(2,1)}), bf16[8,128,256]{2,0,1:T(8,128)(2,1)S(1)}, u32[]{:S(2)}, u32[]{:S(2)}) %all-to-all-start) | async-done | bytes 524320 | tf_op jit(solution)/shard_map/all_to_all | solution.py:389
  39.6 0.0 copy-start
  39.6 0.8 copy-done
  40.4 97.8 %shard_map.95 = (bf16[128,464]{1,0:T(8,128)(2,1)}, s32[2,58]{1,0:T(2,128)}) custom-call(s32[1]{0:T(128)S(6)} %copy.16.count_ref, s32[1,7]{1,0:T(1,128)} %drop_ref.1, s32[1,7]{1,0:T(1,128)} %grow_ref.1, s32[2,58]{1,0:T(2,128)} %old_ref.1, bf16[8,7424]{1,0:T(8,128)(2,1)} %grad_ref.1, bf16[4,4,4,16,256]{4,3,2,1,0:T(8,128)(2,1)} %bitcast.19, ...), custom_call_target="tpu_custom_call" | custom-call | flops 8000000000 | bytes 10000000 | tf_op jit(solution)/shard_map/pallas_call | solution.py:399
  138.2 1.7 %copy.11 = bf16[128,464]{0,1:T(8,128)(2,1)} copy(bf16[128,464]{1,0:T(8,128)(2,1)} %get-tuple-element.2) | data formatting | bytes 237568 | tf_op jit(solution)/shard_map/pallas_call | solution.py:399
  139.9 1.2 copy.17
Async XLA Ops:
  17.8 21.8 %all-to-all-start = ((bf16[8,128,256]{2,0,1:T(8,128)(2,1)}), bf16[8,128,256]{2,0,1:T(8,128)(2,1)S(1)}, u32[]{:S(2)}, u32[]{:S(2)}) async-start(bf16[8,128,256]{2,0,1:T(8,128)(2,1)} %bitcast.17), calls=%async_computation | async-start | bytes 1048576 | tf_op jit(solution)/shard_map/all_to_all | solution.py:389
  39.6 0.8 copy-start

commit v2 on v1

v2 whole, which is shorter than its diff:
```python
import jax
import jax.numpy as jnp
from jax import lax
from jax.experimental import pallas as pl
from jax.experimental.pallas import tpu as pltpu
from jax.sharding import PartitionSpec as P

MESH = pl.DeviceIdType.MESH
BF = jnp.bfloat16
F32 = jnp.float32

RING = 4
ROWS = 16
BLK = 128
HALF = 3712
OWN = 256
CHUNK = 464
PAD = 512

PARTS = (
    ((0, 640, 384), (640, 512, 256)),
    ((1152, 768, 384), (1920, 512, 256)),
    ((2432, 768, 384), (3200, 512, 256)),
)
GROUPS = 2
FAR = (1, 3, 2)
GATHER = (("x", "y", "z"), ("y", "z", "x"), ("z", "x", "y"))
SCATTER = (("x", "y", "z"), ("y", "z", "x"), ("z", "x", "y"))
GDIMS = ("x", "y", "z")
SDIMS = ("z", "x", "y")


def pick(dims, fixed):
    return tuple(fixed[d] if d in fixed else slice(None) for d in dims)


def kernel(
    count_ref, drop_ref, grow_ref, old_ref, grad_ref, hid_ref, inp_ref, w_ref,
    out_ref, mask_ref,
    count, drop, grow, old_v, grad, gm, gp, g, hb, t0, t1, t2, h, ht, acc, w, xin, s, m, expand, ra1, rb1, rb2, rb3, fin, stage, land,
    g_send, g_recv, s_send, s_recv, e_send, e_recv, f_send, f_recv, a_send, a_recv, loc,
):
    fsdp = lax.axis_index("fsdp")
    grp = lax.axis_index("grp")
    me = {"x": fsdp // RING, "y": fsdp % RING, "z": grp // 2}
    core = grp % 2

    def dev(x, y, z, c):
        return (x * RING + y, z * 2 + c)

    def near(axis, step):
        at = dict(me)
        at[axis] = (at[axis] + step) % RING
        return dev(at["x"], at["y"], at["z"], core)

    partner = dev(me["x"], me["y"], me["z"], 1 - core)

    bar = pltpu.get_barrier_semaphore()
    last_core = me["x"] // 2
    self_in = last_core == core
    own_k = (me["x"] % 2) * RING + me["y"]

    def last_dev(k):
        return dev(2 * core + k // RING, k % RING, me["z"], last_core)

    def is_self(k):
        return jnp.logical_and(self_in, own_k == k)

    for axis in ("x", "y", "z"):
        for step in FAR:
            pl.semaphore_signal(bar, inc=1, device_id=near(axis, step), device_id_type=MESH)
    pl.semaphore_signal(bar, inc=1, device_id=partner, device_id_type=MESH)
    for k in range(8):
        @pl.when(jnp.logical_not(is_self(k)))
        def _():
            pl.semaphore_signal(bar, inc=1, device_id=last_dev(k), device_id_type=MESH)

    mine = pl.ds(pl.multiple_of(core * HALF, BLK), HALF)
    other = pl.ds(pl.multiple_of((1 - core) * HALF, BLK), HALF)
    own_rows = pl.ds(pl.multiple_of(core * OWN, OWN), OWN)
    own_tokens = pl.ds(2 * core, 2)

    def slab(z):
        return pl.ds(pl.multiple_of(z * 2 * OWN, 2 * OWN), 2 * OWN)

    local = [
        pltpu.make_async_copy(*pair, loc.at[i])
        for i, pair in enumerate((
            (grad_ref, grad),
            (count_ref, count),
            (hid_ref, hb.at[core]),
            (old_ref, old_v),
            (drop_ref, drop),
            (grow_ref, grow),
            (w_ref.at[:, mine], w.at[own_rows, :]),
            (inp_ref.at[:, :, :, slab(me["z"])], xin.at[me["z"], own_tokens]),
        ))
    ]
    for c in local:
        c.start()

    def remote(src, dst, sends, recvs, i, to):
        return pltpu.make_async_remote_copy(
            src_ref=src, dst_ref=dst, send_sem=sends.at[i], recv_sem=recvs.at[i],
            device_id=to, device_id_type=MESH,
        )

    local[0].wait()
    local[1].wait()
    rows = lax.broadcasted_iota(jnp.int32, grad.shape, 0)
    gm[...] = jnp.where(rows < count[0], grad[...].astype(F32), 0.0).astype(BF)
    gp[core] = gm[:, mine]
    pl.semaphore_wait(bar, jnp.where(self_in, 17, 18))

    swap = [
        remote(gm.at[:, other], gp.at[core], e_send, e_recv, 0, partner),
        remote(hid_ref, hb.at[core], e_send, e_recv, 1, partner),
        remote(m.at[core], m.at[core], e_send, e_recv, 2, partner),
        remote(w_ref.at[:, other], w.at[own_rows, :], e_send, e_recv, 3, partner),
        remote(h.at[core], h.at[core], e_send, e_recv, 4, partner),
        remote(xin.at[:, own_tokens], xin.at[:, own_tokens], e_send, e_recv, 5, partner),
    ]
    swap[0].start()
    swap[1].start()
    swap[3].start()

    inp = [
        remote(
            inp_ref.at[:, :, :, slab((me["z"] + d) % RING)], xin.at[me["z"], own_tokens],
            a_send, a_recv, i, near("z", d),
        )
        for i, d in enumerate(FAR)
    ]
    def hid_step(axis, d):
        v = (me[axis] + d) % RING
        return {
            "x": (t0.at[v], t1.at[me["x"]]),
            "y": (t1.at[:, v], t2.at[:, me["y"]]),
            "z": (t2.at[:, :, v], h.at[core, :, :, me["z"]]),
        }[axis]

    hid = {}
    for q, axis in enumerate(("x", "y", "z")):
        stay = pltpu.make_async_copy(*hid_step(axis, 0), loc.at[8 + q])
        go = [
            remote(*hid_step(axis, d), a_send, a_recv, 3 + q * 3 + i, near(axis, d))
            for i, d in enumerate(FAR)
        ]
        hid[axis] = (stay, go)

    def hid_start(axis):
        for c in (*hid[axis][1], hid[axis][0]):
            c.start()

    def hid_wait(axis):
        hid[axis][0].wait()
        for c in hid[axis][1]:
            c.wait_recv()

    swap[0].wait_recv()
    g[me["x"], me["y"], me["z"]] = jnp.concatenate([gp[0], gp[1]], axis=0)

    sends = []

    def gather_copy(p, q, cols, at, to):
        fixed = {d: me[d] for d in GATHER[p][q:]}
        fixed[GATHER[p][q]] = at
        ref = g.at[(*pick(GDIMS, fixed), slice(None), cols)]
        sends.append(remote(ref, ref, g_send, g_recv, len(sends), to))
        return sends[-1]

    def gather_direct(p, q):
        axis = GATHER[p][q]
        cols = pl.ds(PARTS[p][0][0], sum(n for _, n, _ in PARTS[p]))
        return [gather_copy(p, q, cols, me[axis], near(axis, d)) for d in FAR]

    def gather_ring(p, q, off, width, half):
        axis = GATHER[p][q]
        cols, lo, hi = pl.ds(off, width), pl.ds(off, half), pl.ds(off + half, width - half)
        return [
            gather_copy(p, q, cols, me[axis], near(axis, 1)),
            gather_copy(p, q, cols, me[axis], near(axis, 3)),
            gather_copy(p, q, lo, (me[axis] + 3) % RING, near(axis, 1)),
            gather_copy(p, q, hi, (me[axis] + 1) % RING, near(axis, 3)),
        ]

    g0 = [gather_direct(p, 0) for p in range(3)]
    g1 = [gather_direct(p, 1) for p in range(3)]
    g2 = [[gather_ring(p, 2, *PARTS[p][k]) for p in range(3)] for k in range(GROUPS)]

    def start(copies):
        for c in copies:
            c.start()

    def arrive(copies):
        for c in copies:
            c.wait_recv()

    def tiles(p, k, body):
        off, width, _ = PARTS[p][k]
        whole = width // 256

        def step(t, carry):
            body(pl.multiple_of(off + t * 256, BLK), 256)
            return carry

        lax.fori_loop(0, whole, step, 0)
        if width % 256:
            body(off + whole * 256, width % 256)

    def grad_chunk(p, k, step):
        axis = GATHER[p][2]
        at = (me[axis] + step) % RING
        lhs = ht[p, at]
        sel = pick(GDIMS, {axis: at})

        def body(o, n):
            rhs = g[(*sel, slice(None), pl.ds(o, n))].reshape(256, n)
            part = jnp.dot(lhs, rhs, preferred_element_type=F32)
            if step == 0:
                acc[:, pl.ds(o, n)] = part
            else:
                acc[:, pl.ds(o, n)] += part

        tiles(p, k, body)

    for p in range(3):
        start(g0[p])

    for c in local[3:6]:
        c.wait()
    old = old_v[...]
    ids = lax.broadcasted_iota(jnp.int32, old.shape, 0) * old.shape[1] + lax.broadcasted_iota(
        jnp.int32, old.shape, 1
    )
    new = old
    for i in range(drop.shape[1]):
        new = jnp.where(ids == drop[0, i], 0, new)
    for i in range(grow.shape[1]):
        new = jnp.where(ids == grow[0, i], 1, new)
    mask_ref[...] = new
    m[core] = jnp.zeros((8, BLK), F32)
    m[core, 0:2, 0 : old.shape[1]] = new.astype(F32)
    m[core, 2:4, 0 : old.shape[1]] = (new * old).astype(F32)
    swap[2].start()

    local[2].wait()
    swap[1].wait_recv()

    def sort_hidden(j, carry):
        cols = pl.ds(pl.multiple_of(j * 2 * OWN + core * OWN, OWN), OWN)
        t0[j // 16, j // 4 % 4, j % 4] = jnp.concatenate([hb[0, :, cols], hb[1, :, cols]], axis=0)
        return carry

    lax.fori_loop(0, 64, sort_hidden, 0)
    hid_start("x")
    start(inp)

    def spread(t, carry):
        o = pl.multiple_of(t * BLK, BLK)
        block = lax.broadcasted_iota(jnp.int32, (BLK, BLK), 0) == core * (HALF // BLK) + t
        for i in range(2):
            expand[i, :, pl.ds(o, BLK)] = jnp.dot(
                m[i], block.astype(F32), preferred_element_type=F32
            )
        return carry

    def turn(i, carry):
        for p in range(3):
            sel = pick(GDIMS, {GATHER[p][2]: i})
            for side in range(2):
                part = h[(side, *sel)].reshape(256, OWN)
                ht[p, i, pl.ds(side * OWN, OWN), :] = part.T
        return carry

    for p in range(3):
        arrive(g0[p])
        start(g1[p])
    swap[2].wait_recv()
    lax.fori_loop(0, HALF // BLK, spread, 0)
    hid_wait("x")
    hid_start("y")
    for p in range(3):
        arrive(g1[p])
        start(g2[0][p][:2])
    hid_wait("y")
    hid_start("z")
    local[7].wait()
    arrive(inp)
    swap[5].start()
    hid_wait("z")
    swap[4].start()
    swap[4].wait_recv()
    lax.fori_loop(0, RING, turn, 0)
    for p in range(3):
        for k in range(GROUPS):
            grad_chunk(p, k, 0)
    local[6].wait()
    swap[3].wait_recv()
    swap[5].wait_recv()

    posts = []

    def scatter_copy(p, q, v, cols, into, to):
        fixed = {d: me[d] for d in SCATTER[p][:q]}
        fixed[SCATTER[p][q]] = v
        src = s.at[(*pick(SDIMS, fixed), slice(None), cols)]
        dst = into.at[(*([slice(None)] * (3 - q)), cols)]
        posts.append(remote(src, dst, s_send, s_recv, len(posts), to))
        return posts[-1]

    def scatter_ring(p, off, width, half):
        axis = SCATTER[p][0]
        lo, hi = pl.ds(off, half), pl.ds(off + half, width - half)
        out = []
        for step, cols in ((1, lo), (3, hi)):
            out.append(scatter_copy(p, 0, (me[axis] + 2) % RING, cols, ra1, near(axis, step)))
        for i, (step, cols) in enumerate(((1, hi), (3, lo), (1, lo), (3, hi))):
            v = (me[axis] + step) % RING
            out.append(scatter_copy(p, 0, v, cols, rb1.at[i % 2], near(axis, step)))
        return out

    def scatter_direct(p, q, off, width, half):
        axis = SCATTER[p][q]
        into = (rb2, rb3)[q - 1]
        return [
            scatter_copy(p, q, (me[axis] + d) % RING, pl.ds(off, width), into.at[i], near(axis, d))
            for i, d in enumerate(FAR)
        ]

    s0 = [[scatter_ring(p, *PARTS[p][k]) for p in range(3)] for k in range(GROUPS)]
    s1 = [[scatter_direct(p, 1, *PARTS[p][k]) for p in range(3)] for k in range(GROUPS)]
    s2 = [[scatter_direct(p, 2, *PARTS[p][k]) for p in range(3)] for k in range(GROUPS)]

    def out_chunk(p, k, step):
        axis = SCATTER[p][0]
        sel = pick(SDIMS, {axis: (me[axis] + step) % RING})
        lhs = xin[sel].reshape(256, 2 * OWN)

        def body(o, n):
            cols = pl.ds(o, n)
            part = jnp.dot(lhs, w[:, cols], preferred_element_type=F32)
            s[(*sel, slice(None), cols)] = part.astype(BF).reshape(RING, RING, ROWS, n)

        tiles(p, k, body)

    def update(p, k):
        def body(o, n):
            cols = pl.ds(o, n)
            for r in range(4):
                side, row = r // 2, r % 2
                keep = expand[side, row : row + 1, cols]
                both = expand[side, row + 2 : row + 3, cols]
                span = pl.ds(r * BLK, BLK)
                w[span, cols] = (both * w[span, cols].astype(F32) - keep * acc[span, cols]).astype(BF)

        tiles(p, k, body)

    def add_into(p, q, v, cols, froms):
        fixed = {d: me[d] for d in SCATTER[p][:q]}
        fixed[SCATTER[p][q]] = v
        free = [d for d in SDIMS if d not in fixed]

        def one(lead):
            idx = dict(fixed)
            if free:
                idx[free[0]] = lead
            at = (*pick(SDIMS, idx), slice(None), cols)
            there = ((lead,) if free else ()) + (slice(None),) * (len(free) - 1 if free else 0)
            total = s[at].astype(F32)
            for ref, pre in froms:
                total = total + ref[(*pre, *there, slice(None), cols)].astype(F32)
            return at, total

        if not free:
            return one(None)[1]

        def step(i, carry):
            at, total = one(i)
            s[at] = total.astype(BF)
            return carry

        lax.fori_loop(0, RING, step, 0)
        return None

    def finish(k):
        for p in range(3):
            arrive(g2[k][p][2:])
            grad_chunk(p, k, 2)
            update(p, k)
            out_chunk(p, k, 2)
            start(s0[k][p][:2])

    def sides(k):
        for p in range(3):
            out_chunk(p, k, 1)
            s0[k][p][2].start()
            out_chunk(p, k, 3)
            s0[k][p][3].start()

    def relay(k):
        for p in range(3):
            off, width, half = PARTS[p][k]
            for i, cols in enumerate((pl.ds(off, half), pl.ds(off + half, width - half))):
                s0[k][p][i].wait_recv()
                add_into(p, 0, (me[SCATTER[p][0]] + (1, 3)[i]) % RING, cols, [(ra1, ())])
                s0[k][p][4 + i].start()

    def settle(k):
        for p in range(3):
            off, width, _ = PARTS[p][k]
            arrive(s0[k][p][2:])
            add_into(p, 0, me[SCATTER[p][0]], pl.ds(off, width), [(rb1, (0,)), (rb1, (1,))])
            start(s1[k][p])

    for p in range(3):
        arrive(g2[0][p][:2])
        start(g2[0][p][2:])
        start(g2[1][p][:2])
    for p in range(3):
        grad_chunk(p, 0, 1)
        grad_chunk(p, 0, 3)
    finish(0)
    for p in range(3):
        arrive(g2[1][p][:2])
        start(g2[1][p][2:])
    sides(0)
    for p in range(3):
        grad_chunk(p, 1, 1)
        grad_chunk(p, 1, 3)
    relay(0)
    finish(1)
    sides(1)
    for k in range(GROUPS):
        for p in range(3):
            out_chunk(p, k, 0)
    relay(1)
    settle(0)
    settle(1)
    for k in range(GROUPS):
        for p in range(3):
            off, width, _ = PARTS[p][k]
            arrive(s1[k][p])
            add_into(p, 1, me[SCATTER[p][1]], pl.ds(off, width), [(rb2, (i,)) for i in range(3)])
            start(s2[k][p])
    for k in range(GROUPS):
        for p in range(3):
            off, width, _ = PARTS[p][k]
            arrive(s2[k][p])
            total = add_into(p, 2, me[SCATTER[p][2]], pl.ds(off, width), [(rb3, (i,)) for i in range(3)])
            fin[:, pl.ds(off, width)] = total

    fin[:, pl.ds(HALF, BLK)] = jnp.zeros((ROWS, BLK), F32)
    slot = fsdp % 8
    ends = []
    for k in range(8):
        base, shift = CHUNK * k // BLK * BLK, CHUNK * k % BLK
        piece = fin[:, pl.ds(base, PAD + BLK)]
        if shift:
            piece = pltpu.roll(piece, PAD + BLK - shift, 1)
        stage[k] = piece[:, :PAD].astype(BF)
        away = pltpu.make_async_remote_copy(
            src_ref=stage.at[k], dst_ref=land.at[slot], send_sem=f_send.at[k],
            recv_sem=f_recv.at[slot], device_id=last_dev(k), device_id_type=MESH,
        )
        near_copy = pltpu.make_async_copy(stage.at[k], land.at[slot], f_recv.at[slot])

        @pl.when(jnp.logical_not(is_self(k)))
        def _():
            away.start()

        @pl.when(is_self(k))
        def _():
            near_copy.start()

        ends.append(away)
    for k in range(8):
        pltpu.make_async_copy(stage.at[k], land.at[k], f_recv.at[k]).wait()
        out_ref[pl.ds(k * ROWS, ROWS), :] = land[k][:, :CHUNK]

    for k in range(8):
        @pl.when(jnp.logical_not(is_self(k)))
        def _():
            ends[k].wait_send()
    for c in swap:
        c.wait_send()
    for c in (*sends, *posts):
        c.wait_send()
    for c in (*inp, *hid["x"][1], *hid["y"][1], *hid["z"][1]):
        c.wait_send()


def shards(hidden, grad_out, token_counts, weight, old_mask, drop_list, grow_list, inputs):
    inp = inputs.reshape(2, RING, ROWS, 2048)
    vmem = pl.BlockSpec(memory_space=pltpu.VMEM)
    hbm = pl.BlockSpec(memory_space=pl.ANY)
    dma = pltpu.SemaphoreType.DMA
    cube = (RING, RING, RING, ROWS)
    out, mask = pl.pallas_call(
        kernel,
        out_shape=(
            jax.ShapeDtypeStruct((128, CHUNK), BF),
            jax.ShapeDtypeStruct(old_mask.shape, jnp.int32),
        ),
        in_specs=[hbm] * 8,
        out_specs=(vmem, vmem),
        scratch_shapes=[
            pltpu.SMEM((1,), jnp.int32),
            pltpu.SMEM(drop_list.shape, jnp.int32),
            pltpu.SMEM(grow_list.shape, jnp.int32),
            pltpu.VMEM(old_mask.shape, jnp.int32),
            pltpu.VMEM((8, 2 * HALF), BF),
            pltpu.VMEM((8, 2 * HALF), BF),
            pltpu.VMEM((2, 8, HALF), BF),
            pltpu.VMEM((*cube, HALF), BF),
            pltpu.VMEM((2, 8, 64 * 2 * OWN), BF),
            pltpu.VMEM((*cube, OWN), BF),
            pltpu.VMEM((*cube, OWN), BF),
            pltpu.VMEM((*cube, OWN), BF),
            pltpu.VMEM((2, *cube, OWN), BF),
            pltpu.VMEM((3, RING, 2 * OWN, 256), BF),
            pltpu.VMEM((2 * OWN, HALF), F32),
            pltpu.VMEM((2 * OWN, HALF), BF),
            pltpu.VMEM((*cube, 2 * OWN), BF),
            pltpu.VMEM((*cube, HALF), BF),
            pltpu.VMEM((2, 8, BLK), F32),
            pltpu.VMEM((2, 8, HALF), F32),
            pltpu.VMEM((RING, RING, ROWS, HALF), BF),
            pltpu.VMEM((2, RING, RING, ROWS, HALF), BF),
            pltpu.VMEM((3, RING, ROWS, HALF), BF),
            pltpu.VMEM((3, ROWS, HALF), BF),
            pltpu.VMEM((ROWS, HALF + BLK), F32),
            pltpu.VMEM((8, ROWS, PAD), BF),
            pltpu.VMEM((8, ROWS, PAD), BF),
            dma((42,)), dma((42,)), dma((72,)), dma((72,)), dma((6,)), dma((6,)),
            dma((8,)), dma((8,)), dma((12,)), dma((12,)), dma((11,)),
        ],
        compiler_params=pltpu.CompilerParams(
            collective_id=0, has_side_effects=True, vmem_limit_bytes=60 * 2**20
        ),
        cost_estimate=pl.CostEstimate(flops=8 * 10**9, bytes_accessed=10**7, transcendentals=0),
    )(token_counts, drop_list, grow_list, old_mask, grad_out, hidden, inp, weight)
    return (out, mask)


def solution(mesh):
    split = P(("fsdp", "grp"), None)
    return jax.shard_map(
        shards,
        mesh=mesh,
        in_specs=(split, split, P(("fsdp", "grp")), split, split, split, split, P("grp", "fsdp")),
        out_specs=(P("grp", "fsdp"), split),
        check_vma=False,
    )
```

time: 141 us -> 108 us (0.77)
  blocking collectives: 16.1 us -> 0 us
  waiting for transfers between devices: 13 us -> 0 us
  starting transfers between devices: 8.16 us -> 0 us
  Pallas kernels: 97.8 us -> 103 us
  local copies, waits for them, and re-layouts: 4.79 us -> 2.9 us
    all_to_all x1 -> x0, blocking collectives: 16.1 us -> none  [shards(): lax.all_to_all(inputs.reshape(128, 8, OWN), 'grp', split_axis=1, concat_a...]
    all_to_all x1 -> x0, waiting for transfers between devices: 13 us -> none  [shards(): lax.all_to_all(sections, ('fsdp', 'grp'), split_axis=1, concat_axis=0, ti...]
    all_to_all x1 -> x0, starting transfers between devices: 8.16 us -> none  [shards(): lax.all_to_all(sections, ('fsdp', 'grp'), split_axis=1, concat_axis=0, ti...]
    pallas_call x1, Pallas kernels: 97.8 us -> 103 us  [shards(): pl.pallas_call(kernel, out_shape=(jax.ShapeDtypeStruct((128, CHUNK), BF),...]
  transfers between devices with their start and end apart: 1 -> 0, of which waited for: 1 -> 0; matrix products, arithmetic and copies ran while one was open for 0% -> 0% of each run, Pallas kernels for 0% -> 0%
where the time goes in v2:
time: 108 us; the launch traced here: 107 us
  Pallas kernels  103 us (95%)
  local copies, waits for them, and re-layouts  2.9 us (3%)
  between operations  1.29 us (1%)
    pallas_call x1, Pallas kernels, shards(): pl.pallas_call(kernel, out_shape=(jax.ShapeDtypeStruct((128, CHUNK), BF),...  103 us

profile of v2, /device:TPU:1, one launch (start us, length us, event | category | flops | bytes accessed | tf_op | source)
XLA Modules:
  0.0 107.3 jit_solution(16571126081623889776)
XLA Ops:
  1.3 103.2 %shard_map.95 = (bf16[128,464]{1,0:T(8,128)(2,1)}, s32[2,58]{1,0:T(2,128)}) custom-call(s32[1]{0:T(128)S(6)} %copy.12.count_ref, s32[1,7]{1,0:T(1,128)} %drop_ref.1, s32[1,7]{1,0:T(1,128)} %grow_ref.1, s32[2,58]{1,0:T(2,128)} %old_ref.1, bf16[8,7424]{1,0:T(8,128)(2,1)} %grad_ref.1, bf16[8,32768]{1,0:T(8,128)(2,1)} %hid_ref.1, ...), custom_call_target="tpu_custom_call" | custom-call | flops 8000000000 | bytes 10000000 | tf_op jit(solution)/shard_map/pallas_call | solution.py:499
  104.4 1.7 %copy.10 = bf16[128,464]{0,1:T(8,128)(2,1)} copy(bf16[128,464]{1,0:T(8,128)(2,1)} %get-tuple-element.2) | data formatting | bytes 237568 | tf_op jit(solution)/shard_map/pallas_call | solution.py:499
  106.1 1.2 %copy.13 = s32[2,58]{1,0:T(2,128)} copy(s32[2,58]{1,0:T(2,128)} %get-tuple-element.7) | data formatting | bytes 928

commit v3 on v2

--- a/solution.py
+++ b/solution.py
@@ -18,12 +18,13 @@
 PAD = 512
 
 PARTS = (
-    ((0, 640, 384), (640, 512, 256)),
-    ((1152, 768, 384), (1920, 512, 256)),
-    ((2432, 768, 384), (3200, 512, 256)),
+    ((0, 640, 384), (2176, 512, 256)),
+    ((640, 768, 384), (2688, 512, 256)),
+    ((1408, 768, 384), (3200, 512, 256)),
 )
 GROUPS = 2
 FAR = (1, 3, 2)
+TURNS = (("x", "y", "z"), ("y", "z", "x"))
 GATHER = (("x", "y", "z"), ("y", "z", "x"), ("z", "x", "y"))
 SCATTER = (("x", "y", "z"), ("y", "z", "x"), ("z", "x", "y"))
 GDIMS = ("x", "y", "z")
@@ -70,11 +71,6 @@
         for step in FAR:
             pl.semaphore_signal(bar, inc=1, device_id=near(axis, step), device_id_type=MESH)
     pl.semaphore_signal(bar, inc=1, device_id=partner, device_id_type=MESH)
-    for k in range(8):
-        @pl.when(jnp.logical_not(is_self(k)))
-        def _():
-            pl.semaphore_signal(bar, inc=1, device_id=last_dev(k), device_id_type=MESH)
-
     mine = pl.ds(pl.multiple_of(core * HALF, BLK), HALF)
     other = pl.ds(pl.multiple_of((1 - core) * HALF, BLK), HALF)
     own_rows = pl.ds(pl.multiple_of(core * OWN, OWN), OWN)
@@ -110,7 +106,7 @@
     rows = lax.broadcasted_iota(jnp.int32, grad.shape, 0)
     gm[...] = jnp.where(rows < count[0], grad[...].astype(F32), 0.0).astype(BF)
     gp[core] = gm[:, mine]
-    pl.semaphore_wait(bar, jnp.where(self_in, 17, 18))
+    pl.semaphore_wait(bar, 10)
 
     swap = [
         remote(gm.at[:, other], gp.at[core], e_send, e_recv, 0, partner),
@@ -131,31 +127,34 @@
         )
         for i, d in enumerate(FAR)
     ]
-    def hid_step(axis, d):
-        v = (me[axis] + d) % RING
-        return {
-            "x": (t0.at[v], t1.at[me["x"]]),
-            "y": (t1.at[:, v], t2.at[:, me["y"]]),
-            "z": (t2.at[:, :, v], h.at[core, :, :, me["z"]]),
-        }[axis]
-
-    hid = {}
-    for q, axis in enumerate(("x", "y", "z")):
-        stay = pltpu.make_async_copy(*hid_step(axis, 0), loc.at[8 + q])
-        go = [
-            remote(*hid_step(axis, d), a_send, a_recv, 3 + q * 3 + i, near(axis, d))
-            for i, d in enumerate(FAR)
-        ]
-        hid[axis] = (stay, go)
-
-    def hid_start(axis):
-        for c in (*hid[axis][1], hid[axis][0]):
-            c.start()
-
-    def hid_wait(axis):
-        hid[axis][0].wait()
-        for c in hid[axis][1]:
-            c.wait_recv()
+    hid = []
+    for u in range(2):
+        for q, axis in enumerate(TURNS[u]):
+            src = (t0, t1, t2)[q].at[u]
+            dst = (t1.at[u], t2.at[u], h.at[core, u])[q]
+
+            def ends_of(d):
+                v = (me[axis] + d) % RING
+                return src.at[pick(GDIMS, {axis: v})], dst.at[pick(GDIMS, {axis: me[axis]})]
+
+            n = u * 3 + q
+            stay = pltpu.make_async_copy(*ends_of(0), loc.at[8 + n])
+            go = [
+                remote(*ends_of(d), a_send, a_recv, 3 + n * 3 + i, near(axis, d))
+                for i, d in enumerate(FAR)
+            ]
+            hid.append((stay, go))
+
+    def hid_start(q):
+        for u in range(2):
+            for c in (*hid[u * 3 + q][1], hid[u * 3 + q][0]):
+                c.start()
+
+    def hid_wait(q):
+        for u in range(2):
+            hid[u * 3 + q][0].wait()
+            for c in hid[u * 3 + q][1]:
+                c.wait_recv()
 
     swap[0].wait_recv()
     g[me["x"], me["y"], me["z"]] = jnp.concatenate([gp[0], gp[1]], axis=0)
@@ -169,9 +168,9 @@
         sends.append(remote(ref, ref, g_send, g_recv, len(sends), to))
         return sends[-1]
 
-    def gather_direct(p, q):
+    def gather_direct(p, q, off, width, half):
         axis = GATHER[p][q]
-        cols = pl.ds(PARTS[p][0][0], sum(n for _, n, _ in PARTS[p]))
+        cols = pl.ds(off, width)
         return [gather_copy(p, q, cols, me[axis], near(axis, d)) for d in FAR]
 
     def gather_ring(p, q, off, width, half):
@@ -184,8 +183,8 @@
             gather_copy(p, q, hi, (me[axis] + 1) % RING, near(axis, 3)),
         ]
 
-    g0 = [gather_direct(p, 0) for p in range(3)]
-    g1 = [gather_direct(p, 1) for p in range(3)]
+    g0 = [[gather_direct(p, 0, *PARTS[p][k]) for p in range(3)] for k in range(GROUPS)]
+    g1 = [[gather_direct(p, 1, *PARTS[p][k]) for p in range(3)] for k in range(GROUPS)]
     g2 = [[gather_ring(p, 2, *PARTS[p][k]) for p in range(3)] for k in range(GROUPS)]
 
     def start(copies):
@@ -195,37 +194,23 @@
     def arrive(copies):
         for c in copies:
             c.wait_recv()
-
-    def tiles(p, k, body):
-        off, width, _ = PARTS[p][k]
-        whole = width // 256
-
-        def step(t, carry):
-            body(pl.multiple_of(off + t * 256, BLK), 256)
-            return carry
-
-        lax.fori_loop(0, whole, step, 0)
-        if width % 256:
-            body(off + whole * 256, width % 256)
 
     def grad_chunk(p, k, step):
         axis = GATHER[p][2]
         at = (me[axis] + step) % RING
         lhs = ht[p, at]
-        sel = pick(GDIMS, {axis: at})
-
-        def body(o, n):
-            rhs = g[(*sel, slice(None), pl.ds(o, n))].reshape(256, n)
-            part = jnp.dot(lhs, rhs, preferred_element_type=F32)
-            if step == 0:
-                acc[:, pl.ds(o, n)] = part
-            else:
-                acc[:, pl.ds(o, n)] += part
-
-        tiles(p, k, body)
-
-    for p in range(3):
-        start(g0[p])
+        off, width, _ = PARTS[p][k]
+        cols = pl.ds(off, width)
+        rhs = g[(*pick(GDIMS, {axis: at}), slice(None), cols)].reshape(256, width)
+        part = jnp.dot(lhs, rhs, preferred_element_type=F32)
+        if step == 0:
+            acc[:, cols] = part
+        else:
+            acc[:, cols] += part
+
+    for k in range(GROUPS):
+        for p in range(3):
+            start(g0[k][p])
 
     for c in local[3:6]:
         c.wait()
@@ -248,12 +233,14 @@
     swap[1].wait_recv()
 
     def sort_hidden(j, carry):
-        cols = pl.ds(pl.multiple_of(j * 2 * OWN + core * OWN, OWN), OWN)
-        t0[j // 16, j // 4 % 4, j % 4] = jnp.concatenate([hb[0, :, cols], hb[1, :, cols]], axis=0)
+        for u in range(2):
+            cols = pl.ds(pl.multiple_of(j * 2 * OWN + core * OWN + u * BLK, BLK), BLK)
+            both = jnp.concatenate([hb[0, :, cols], hb[1, :, cols]], axis=0)
+            t0[u, j // 16, j // 4 % 4, j % 4] = both
         return carry
 
     lax.fori_loop(0, 64, sort_hidden, 0)
-    hid_start("x")
+    hid_start(0)
     start(inp)
 
     def spread(t, carry):
@@ -268,32 +255,39 @@
     def turn(i, carry):
         for p in range(3):
             sel = pick(GDIMS, {GATHER[p][2]: i})
-            for side in range(2):
-                part = h[(side, *sel)].reshape(256, OWN)
-                ht[p, i, pl.ds(side * OWN, OWN), :] = part.T
+            for n in range(4):
+                part = h[(n // 2, n % 2, *sel)].reshape(256, BLK)
+                ht[p, i, pl.ds(n * BLK, BLK), :] = part.T
         return carry
 
-    for p in range(3):
-        arrive(g0[p])
-        start(g1[p])
+    for k in range(GROUPS):
+        for p in range(3):
+            arrive(g0[k][p])
+            start(g1[k][p])
+    hid_wait(0)
+    hid_start(1)
     swap[2].wait_recv()
     lax.fori_loop(0, HALF // BLK, spread, 0)
-    hid_wait("x")
-    hid_start("y")
     for p in range(3):
-        arrive(g1[p])
+        arrive(g1[0][p])
         start(g2[0][p][:2])
-    hid_wait("y")
-    hid_start("z")
+    hid_wait(1)
+    hid_start(2)
+    for p in range(3):
+        arrive(g1[1][p])
     local[7].wait()
     arrive(inp)
     swap[5].start()
-    hid_wait("z")
+    for p in range(3):
+        arrive(g2[0][p][:2])
+        start(g2[0][p][2:])
+        start(g2[1][p][:2])
+    hid_wait(2)
     swap[4].start()
     swap[4].wait_recv()
     lax.fori_loop(0, RING, turn, 0)
-    for p in range(3):
-        for k in range(GROUPS):
+    for k in range(GROUPS):
+        for p in range(3):
             grad_chunk(p, k, 0)
     local[6].wait()
     swap[3].wait_recv()
@@ -335,26 +329,20 @@
     def out_chunk(p, k, step):
         axis = SCATTER[p][0]
         sel = pick(SDIMS, {axis: (me[axis] + step) % RING})
-        lhs = xin[sel].reshape(256, 2 * OWN)
-
-        def body(o, n):
-            cols = pl.ds(o, n)
-            part = jnp.dot(lhs, w[:, cols], preferred_element_type=F32)
-            s[(*sel, slice(None), cols)] = part.astype(BF).reshape(RING, RING, ROWS, n)
-
-        tiles(p, k, body)
+        off, width, _ = PARTS[p][k]
+        cols = pl.ds(off, width)
+        part = jnp.dot(xin[sel].reshape(256, 2 * OWN), w[:, cols], preferred_element_type=F32)
+        s[(*sel, slice(None), cols)] = part.astype(BF).reshape(RING, RING, ROWS, width)
 
     def update(p, k):
-        def body(o, n):
-            cols = pl.ds(o, n)
-            for r in range(4):
-                side, row = r // 2, r % 2
-                keep = expand[side, row : row + 1, cols]
-                both = expand[side, row + 2 : row + 3, cols]
-                span = pl.ds(r * BLK, BLK)
-                w[span, cols] = (both * w[span, cols].astype(F32) - keep * acc[span, cols]).astype(BF)
-
-        tiles(p, k, body)
+        off, width, _ = PARTS[p][k]
+        cols = pl.ds(off, width)
+        for r in range(4):
+            side, row = r // 2, r % 2
+            keep = expand[side, row : row + 1, cols]
+            both = expand[side, row + 2 : row + 3, cols]
+            span = pl.ds(r * BLK, BLK)
+            w[span, cols] = (both * w[span, cols].astype(F32) - keep * acc[span, cols]).astype(BF)
 
     def add_into(p, q, v, cols, froms):
         fixed = {d: me[d] for d in SCATTER[p][:q]}
@@ -413,10 +401,6 @@
             add_into(p, 0, me[SCATTER[p][0]], pl.ds(off, width), [(rb1, (0,)), (rb1, (1,))])
             start(s1[k][p])
 
-    for p in range(3):
-        arrive(g2[0][p][:2])
-        start(g2[0][p][2:])
-        start(g2[1][p][:2])
     for p in range(3):
         grad_chunk(p, 0, 1)
         grad_chunk(p, 0, 3)
@@ -443,17 +427,10 @@
             arrive(s1[k][p])
             add_into(p, 1, me[SCATTER[p][1]], pl.ds(off, width), [(rb2, (i,)) for i in range(3)])
             start(s2[k][p])
-    for k in range(GROUPS):
-        for p in range(3):
-            off, width, _ = PARTS[p][k]
-            arrive(s2[k][p])
-            total = add_into(p, 2, me[SCATTER[p][2]], pl.ds(off, width), [(rb3, (i,)) for i in range(3)])
-            fin[:, pl.ds(off, width)] = total
-
-    fin[:, pl.ds(HALF, BLK)] = jnp.zeros((ROWS, BLK), F32)
     slot = fsdp % 8
     ends = []
-    for k in range(8):
+
+    def deliver(k):
         base, shift = CHUNK * k // BLK * BLK, CHUNK * k % BLK
         piece = fin[:, pl.ds(base, PAD + BLK)]
         if shift:
@@ -463,7 +440,6 @@
             src_ref=stage.at[k], dst_ref=land.at[slot], send_sem=f_send.at[k],
             recv_sem=f_recv.at[slot], device_id=last_dev(k), device_id_type=MESH,
         )
-        near_copy = pltpu.make_async_copy(stage.at[k], land.at[slot], f_recv.at[slot])
 
         @pl.when(jnp.logical_not(is_self(k)))
         def _():
@@ -471,9 +447,19 @@
 
         @pl.when(is_self(k))
         def _():
-            near_copy.start()
+            pltpu.make_async_copy(stage.at[k], land.at[slot], f_recv.at[slot]).start()
 
         ends.append(away)
+
+    fin[:, pl.ds(HALF, BLK)] = jnp.zeros((ROWS, BLK), F32)
+    for k in range(GROUPS):
+        for p in range(3):
+            off, width, _ = PARTS[p][k]
+            arrive(s2[k][p])
+            total = add_into(p, 2, me[SCATTER[p][2]], pl.ds(off, width), [(rb3, (i,)) for i in range(3)])
+            fin[:, pl.ds(off, width)] = total
+        for n in range(4 * k, 4 * k + 4):
+            deliver(n)
     for k in range(8):
         pltpu.make_async_copy(stage.at[k], land.at[k], f_recv.at[k]).wait()
         out_ref[pl.ds(k * ROWS, ROWS), :] = land[k][:, :CHUNK]
@@ -486,7 +472,7 @@
         c.wait_send()
     for c in (*sends, *posts):
         c.wait_send()
-    for c in (*inp, *hid["x"][1], *hid["y"][1], *hid["z"][1]):
+    for c in (*inp, *(c for pair in hid for c in pair[1])):
         c.wait_send()
 
 
@@ -514,10 +500,10 @@
             pltpu.VMEM((2, 8, HALF), BF),
             pltpu.VMEM((*cube, HALF), BF),
             pltpu.VMEM((2, 8, 64 * 2 * OWN), BF),
-            pltpu.VMEM((*cube, OWN), BF),
-            pltpu.VMEM((*cube, OWN), BF),
-            pltpu.VMEM((*cube, OWN), BF),
-            pltpu.VMEM((2, *cube, OWN), BF),
+            pltpu.VMEM((2, *cube, BLK), BF),
+            pltpu.VMEM((2, *cube, BLK), BF),
+            pltpu.VMEM((2, *cube, BLK), BF),
+            pltpu.VMEM((2, 2, *cube, BLK), BF),
             pltpu.VMEM((3, RING, 2 * OWN, 256), BF),
             pltpu.VMEM((2 * OWN, HALF), F32),
             pltpu.VMEM((2 * OWN, HALF), BF),
@@ -532,8 +518,8 @@
             pltpu.VMEM((ROWS, HALF + BLK), F32),
             pltpu.VMEM((8, ROWS, PAD), BF),
             pltpu.VMEM((8, ROWS, PAD), BF),
-            dma((42,)), dma((42,)), dma((72,)), dma((72,)), dma((6,)), dma((6,)),
-            dma((8,)), dma((8,)), dma((12,)), dma((12,)), dma((11,)),
+            dma((60,)), dma((60,)), dma((72,)), dma((72,)), dma((6,)), dma((6,)),
+            dma((8,)), dma((8,)), dma((21,)), dma((21,)), dma((14,)),
         ],
         compiler_params=pltpu.CompilerParams(
             collective_id=0, has_side_effects=True, vmem_limit_bytes=60 * 2**20

time: 108 us -> 96.6 us (0.89)
  Pallas kernels: 103 us -> 91.6 us
    pallas_call x1, Pallas kernels: 103 us -> 91.6 us  [shards(): pl.pallas_call(kernel, out_shape=(jax.ShapeDtypeStruct((128, CHUNK), BF),...]
where the time goes in v3:
time: 96.6 us; the launch traced here: 95.8 us
  Pallas kernels  91.6 us (95%)
  local copies, waits for them, and re-layouts  2.9 us (3%)
  between operations  1.29 us (1%)
    pallas_call x1, Pallas kernels, shards(): pl.pallas_call(kernel, out_shape=(jax.ShapeDtypeStruct((128, CHUNK), BF),...  91.6 us

profile of v3, /device:TPU:1, one launch (start us, length us, event | category | flops | bytes accessed | tf_op | source)
XLA Modules:
  0.0 95.8 jit_solution(16343593241939691700)
XLA Ops:
  1.3 91.6 %shard_map.95 = (bf16[128,464]{1,0:T(8,128)(2,1)}, s32[2,58]{1,0:T(2,128)}) custom-call(s32[1]{0:T(128)S(6)} %copy.12.count_ref, s32[1,7]{1,0:T(1,128)} %drop_ref.1, s32[1,7]{1,0:T(1,128)} %grow_ref.1, s32[2,58]{1,0:T(2,128)} %old_ref.1, bf16[8,7424]{1,0:T(8,128)(2,1)} %grad_ref.1, bf16[8,32768]{1,0:T(8,128)(2,1)} %hid_ref.1, ...), custom_call_target="tpu_custom_call" | custom-call | flops 8000000000 | bytes 10000000 | tf_op jit(solution)/shard_map/pallas_call | solution.py:485
  92.9 1.7 %copy.10 = bf16[128,464]{0,1:T(8,128)(2,1)} copy(bf16[128,464]{1,0:T(8,128)(2,1)} %get-tuple-element.2) | data formatting | bytes 237568 | tf_op jit(solution)/shard_map/pallas_call | solution.py:485
  94.6 1.2 %copy.13 = s32[2,58]{1,0:T(2,128)} copy(s32[2,58]{1,0:T(2,128)} %get-tuple-element.7) | data formatting | bytes 928

commit v4 on v3

--- a/solution.py
+++ b/solution.py
@@ -95,11 +95,14 @@
     for c in local:
         c.start()
 
-    def remote(src, dst, sends, recvs, i, to):
+    def remote(src, dst, send, recv, to):
         return pltpu.make_async_remote_copy(
-            src_ref=src, dst_ref=dst, send_sem=sends.at[i], recv_sem=recvs.at[i],
+            src_ref=src, dst_ref=dst, send_sem=send, recv_sem=recv,
             device_id=to, device_id_type=MESH,
         )
+
+    def wait_for(like, sem):
+        pltpu.make_async_copy(like, like, sem).wait()
 
     local[0].wait()
     local[1].wait()
@@ -109,12 +112,12 @@
     pl.semaphore_wait(bar, 10)
 
     swap = [
-        remote(gm.at[:, other], gp.at[core], e_send, e_recv, 0, partner),
-        remote(hid_ref, hb.at[core], e_send, e_recv, 1, partner),
-        remote(m.at[core], m.at[core], e_send, e_recv, 2, partner),
-        remote(w_ref.at[:, other], w.at[own_rows, :], e_send, e_recv, 3, partner),
-        remote(h.at[core], h.at[core], e_send, e_recv, 4, partner),
-        remote(xin.at[:, own_tokens], xin.at[:, own_tokens], e_send, e_recv, 5, partner),
+        remote(gm.at[:, other], gp.at[core], e_send.at[0], e_recv.at[0], partner),
+        remote(hid_ref, hb.at[core], e_send.at[1], e_recv.at[1], partner),
+        remote(m.at[core], m.at[core], e_send.at[2], e_recv.at[2], partner),
+        remote(w_ref.at[:, other], w.at[own_rows, :], e_send.at[3], e_recv.at[3], partner),
+        remote(h.at[core], h.at[core], e_send.at[4], e_recv.at[4], partner),
+        remote(xin.at[:, own_tokens], xin.at[:, own_tokens], e_send.at[5], e_recv.at[5], partner),
     ]
     swap[0].start()
     swap[1].start()
@@ -123,9 +126,9 @@
     inp = [
         remote(
             inp_ref.at[:, :, :, slab((me["z"] + d) % RING)], xin.at[me["z"], own_tokens],
-            a_send, a_recv, i, near("z", d),
+            a_send.at[3], a_recv.at[3], near("z", d),
         )
-        for i, d in enumerate(FAR)
+        for d in FAR
     ]
     hid = []
     for u in range(2):
@@ -137,12 +140,8 @@
                 v = (me[axis] + d) % RING
                 return src.at[pick(GDIMS, {axis: v})], dst.at[pick(GDIMS, {axis: me[axis]})]
 
-            n = u * 3 + q
-            stay = pltpu.make_async_copy(*ends_of(0), loc.at[8 + n])
-            go = [
-                remote(*ends_of(d), a_send, a_recv, 3 + n * 3 + i, near(axis, d))
-                for i, d in enumerate(FAR)
-            ]
+            stay = pltpu.make_async_copy(*ends_of(0), loc.at[8 + u * 3 + q])
+            go = [remote(*ends_of(d), a_send.at[q], a_recv.at[q], near(axis, d)) for d in FAR]
             hid.append((stay, go))
 
     def hid_start(q):
@@ -153,47 +152,50 @@
     def hid_wait(q):
         for u in range(2):
             hid[u * 3 + q][0].wait()
-            for c in hid[u * 3 + q][1]:
-                c.wait_recv()
+        wait_for(t0.at[:, 0:3], a_recv.at[q])
 
     swap[0].wait_recv()
     g[me["x"], me["y"], me["z"]] = jnp.concatenate([gp[0], gp[1]], axis=0)
 
-    sends = []
-
-    def gather_copy(p, q, cols, at, to):
+    def gather_copy(p, q, cols, at, to, send, recv):
         fixed = {d: me[d] for d in GATHER[p][q:]}
         fixed[GATHER[p][q]] = at
         ref = g.at[(*pick(GDIMS, fixed), slice(None), cols)]
-        sends.append(remote(ref, ref, g_send, g_recv, len(sends), to))
-        return sends[-1]
-
-    def gather_direct(p, q, off, width, half):
+        return remote(ref, ref, g_send.at[send], g_recv.at[recv], to)
+
+    def gather_direct(k, p, q):
+        off, width, _ = PARTS[p][k]
         axis = GATHER[p][q]
+        cols, n = pl.ds(off, width), q * 6 + k * 3 + p
+        return [gather_copy(p, q, cols, me[axis], near(axis, d), q, n) for d in FAR]
+
+    def gather_ring(k, p):
+        off, width, half = PARTS[p][k]
+        axis = GATHER[p][2]
+        cols, lo, hi = pl.ds(off, width), pl.ds(off, half), pl.ds(off + half, width - half)
+        n = 12 + k * 3 + p
+        return [
+            gather_copy(p, 2, cols, me[axis], near(axis, 1), 2, n),
+            gather_copy(p, 2, cols, me[axis], near(axis, 3), 2, n),
+            gather_copy(p, 2, lo, (me[axis] + 3) % RING, near(axis, 1), 3, n + 6),
+            gather_copy(p, 2, hi, (me[axis] + 1) % RING, near(axis, 3), 3, n + 6),
+        ]
+
+    g0 = [[gather_direct(k, p, 0) for p in range(3)] for k in range(GROUPS)]
+    g1 = [[gather_direct(k, p, 1) for p in range(3)] for k in range(GROUPS)]
+    g2 = [[gather_ring(k, p) for p in range(3)] for k in range(GROUPS)]
+
+    def gathered(k, p, q):
+        off, width, _ = PARTS[p][k]
         cols = pl.ds(off, width)
-        return [gather_copy(p, q, cols, me[axis], near(axis, d)) for d in FAR]
-
-    def gather_ring(p, q, off, width, half):
-        axis = GATHER[p][q]
-        cols, lo, hi = pl.ds(off, width), pl.ds(off, half), pl.ds(off + half, width - half)
-        return [
-            gather_copy(p, q, cols, me[axis], near(axis, 1)),
-            gather_copy(p, q, cols, me[axis], near(axis, 3)),
-            gather_copy(p, q, lo, (me[axis] + 3) % RING, near(axis, 1)),
-            gather_copy(p, q, hi, (me[axis] + 1) % RING, near(axis, 3)),
-        ]
-
-    g0 = [[gather_direct(p, 0, *PARTS[p][k]) for p in range(3)] for k in range(GROUPS)]
-    g1 = [[gather_direct(p, 1, *PARTS[p][k]) for p in range(3)] for k in range(GROUPS)]
-    g2 = [[gather_ring(p, 2, *PARTS[p][k]) for p in range(3)] for k in range(GROUPS)]
+        like = (
+            rb3.at[:, :, cols], rb2.at[:, :, :, cols], rb1.at[:, :, :, :, cols], ra1.at[:, :, :, cols]
+        )[q]
+        wait_for(like, g_recv.at[q * 6 + k * 3 + p])
 
     def start(copies):
         for c in copies:
             c.start()
-
-    def arrive(copies):
-        for c in copies:
-            c.wait_recv()
 
     def grad_chunk(p, k, step):
         axis = GATHER[p][2]
@@ -262,24 +264,24 @@
 
     for k in range(GROUPS):
         for p in range(3):
-            arrive(g0[k][p])
+            gathered(k, p, 0)
             start(g1[k][p])
     hid_wait(0)
     hid_start(1)
     swap[2].wait_recv()
     lax.fori_loop(0, HALF // BLK, spread, 0)
     for p in range(3):
-        arrive(g1[0][p])
+        gathered(0, p, 1)
         start(g2[0][p][:2])
     hid_wait(1)
     hid_start(2)
     for p in range(3):
-        arrive(g1[1][p])
+        gathered(1, p, 1)
     local[7].wait()
-    arrive(inp)
+    wait_for(xin.at[0:3, own_tokens], a_recv.at[3])
     swap[5].start()
     for p in range(3):
-        arrive(g2[0][p][:2])
+        gathered(0, p, 2)
         start(g2[0][p][2:])
         start(g2[1][p][:2])
     hid_wait(2)
@@ -293,38 +295,46 @@
     swap[3].wait_recv()
     swap[5].wait_recv()
 
-    posts = []
-
-    def scatter_copy(p, q, v, cols, into, to):
+    def scatter_copy(p, q, v, cols, into, to, send, recv):
         fixed = {d: me[d] for d in SCATTER[p][:q]}
         fixed[SCATTER[p][q]] = v
         src = s.at[(*pick(SDIMS, fixed), slice(None), cols)]
         dst = into.at[(*([slice(None)] * (3 - q)), cols)]
-        posts.append(remote(src, dst, s_send, s_recv, len(posts), to))
-        return posts[-1]
-
-    def scatter_ring(p, off, width, half):
+        return remote(src, dst, s_send.at[send], s_recv.at[recv], to)
+
+    def scatter_ring(k, p):
+        off, width, half = PARTS[p][k]
         axis = SCATTER[p][0]
-        lo, hi = pl.ds(off, half), pl.ds(off + half, width - half)
+        lo, hi, n = pl.ds(off, half), pl.ds(off + half, width - half), k * 3 + p
         out = []
         for step, cols in ((1, lo), (3, hi)):
-            out.append(scatter_copy(p, 0, (me[axis] + 2) % RING, cols, ra1, near(axis, step)))
+            v = (me[axis] + 2) % RING
+            out.append(scatter_copy(p, 0, v, cols, ra1, near(axis, step), 0, n))
         for i, (step, cols) in enumerate(((1, hi), (3, lo), (1, lo), (3, hi))):
             v = (me[axis] + step) % RING
-            out.append(scatter_copy(p, 0, v, cols, rb1.at[i % 2], near(axis, step)))
+            out.append(scatter_copy(p, 0, v, cols, rb1.at[i % 2], near(axis, step), 1, 6 + n))
         return out
 
-    def scatter_direct(p, q, off, width, half):
+    def scatter_direct(k, p, q):
+        off, width, _ = PARTS[p][k]
         axis = SCATTER[p][q]
-        into = (rb2, rb3)[q - 1]
+        into, cols, n = (rb2, rb3)[q - 1], pl.ds(off, width), 6 + q * 6 + k * 3 + p
         return [
-            scatter_copy(p, q, (me[axis] + d) % RING, pl.ds(off, width), into.at[i], near(axis, d))
+            scatter_copy(p, q, (me[axis] + d) % RING, cols, into.at[i], near(axis, d), 1 + q, n)
             for i, d in enumerate(FAR)
         ]
 
-    s0 = [[scatter_ring(p, *PARTS[p][k]) for p in range(3)] for k in range(GROUPS)]
-    s1 = [[scatter_direct(p, 1, *PARTS[p][k]) for p in range(3)] for k in range(GROUPS)]
-    s2 = [[scatter_direct(p, 2, *PARTS[p][k]) for p in range(3)] for k in range(GROUPS)]
+    s0 = [[scatter_ring(k, p) for p in range(3)] for k in range(GROUPS)]
+    s1 = [[scatter_direct(k, p, 1) for p in range(3)] for k in range(GROUPS)]
+    s2 = [[scatter_direct(k, p, 2) for p in range(3)] for k in range(GROUPS)]
+
+    def scattered(k, p, q):
+        off, width, _ = PARTS[p][k]
+        cols = pl.ds(off, width)
+        like = (
+            ra1.at[:, :, :, cols], rb1.at[:, :, :, :, cols], rb2.at[:, :, :, cols], rb3.at[:, :, cols]
+        )[q]
+        wait_for(like, s_recv.at[q * 6 + k * 3 + p])
 
     def out_chunk(p, k, step):
         axis = SCATTER[p][0]
@@ -373,7 +383,7 @@
 
     def finish(k):
         for p in range(3):
-            arrive(g2[k][p][2:])
+            gathered(k, p, 3)
             grad_chunk(p, k, 2)
             update(p, k)
             out_chunk(p, k, 2)
@@ -389,15 +399,15 @@
     def relay(k):
         for p in range(3):
             off, width, half = PARTS[p][k]
+            scattered(k, p, 0)
             for i, cols in enumerate((pl.ds(off, half), pl.ds(off + half, width - half))):
-                s0[k][p][i].wait_recv()
                 add_into(p, 0, (me[SCATTER[p][0]] + (1, 3)[i]) % RING, cols, [(ra1, ())])
                 s0[k][p][4 + i].start()
 
     def settle(k):
         for p in range(3):
             off, width, _ = PARTS[p][k]
-            arrive(s0[k][p][2:])
+            scattered(k, p, 1)
             add_into(p, 0, me[SCATTER[p][0]], pl.ds(off, width), [(rb1, (0,)), (rb1, (1,))])
             start(s1[k][p])
 
@@ -406,7 +416,7 @@
         grad_chunk(p, 0, 3)
     finish(0)
     for p in range(3):
-        arrive(g2[1][p][:2])
+        gathered(1, p, 2)
         start(g2[1][p][2:])
     sides(0)
     for p in range(3):
@@ -424,7 +434,7 @@
     for k in range(GROUPS):
         for p in range(3):
             off, width, _ = PARTS[p][k]
-            arrive(s1[k][p])
+            scattered(k, p, 2)
             add_into(p, 1, me[SCATTER[p][1]], pl.ds(off, width), [(rb2, (i,)) for i in range(3)])
             start(s2[k][p])
     slot = fsdp % 8
@@ -455,7 +465,7 @@
     for k in range(GROUPS):
         for p in range(3):
             off, width, _ = PARTS[p][k]
-            arrive(s2[k][p])
+            scattered(k, p, 3)
             total = add_into(p, 2, me[SCATTER[p][2]], pl.ds(off, width), [(rb3, (i,)) for i in range(3)])
             fin[:, pl.ds(off, width)] = total
         for n in range(4 * k, 4 * k + 4):
@@ -470,10 +480,13 @@
             ends[k].wait_send()
     for c in swap:
         c.wait_send()
-    for c in (*sends, *posts):
-        c.wait_send()
-    for c in (*inp, *(c for pair in hid for c in pair[1])):
-        c.wait_send()
+    for i, like in enumerate((rb3, rb2, rb1, ra1)):
+        wait_for(like, g_send.at[i])
+    for i, like in enumerate((ra1, rb1, rb2, rb3)):
+        wait_for(like, s_send.at[i])
+    for i in range(3):
+        wait_for(t0.at[:, 0:3], a_send.at[i])
+    wait_for(xin.at[0:3, own_tokens], a_send.at[3])
 
 
 def shards(hidden, grad_out, token_counts, weight, old_mask, drop_list, grow_list, inputs):
@@ -518,8 +531,8 @@
             pltpu.VMEM((ROWS, HALF + BLK), F32),
             pltpu.VMEM((8, ROWS, PAD), BF),
             pltpu.VMEM((8, ROWS, PAD), BF),
-            dma((60,)), dma((60,)), dma((72,)), dma((72,)), dma((6,)), dma((6,)),
-            dma((8,)), dma((8,)), dma((21,)), dma((21,)), dma((14,)),
+            dma((4,)), dma((24,)), dma((4,)), dma((24,)), dma((6,)), dma((6,)),
+            dma((8,)), dma((8,)), dma((4,)), dma((4,)), dma((14,)),
         ],
         compiler_params=pltpu.CompilerParams(
             collective_id=0, has_side_effects=True, vmem_limit_bytes=60 * 2**20

time: 96.6 us -> 94.1 us (0.974)
  Pallas kernels: 91.6 us -> 89.1 us
    pallas_call x1, Pallas kernels: 91.6 us -> 89.1 us  [shards(): pl.pallas_call(kernel, out_shape=(jax.ShapeDtypeStruct((128, CHUNK), BF),...]
where the time goes in v4:
time: 94.1 us; the launch traced here: 93.3 us
  Pallas kernels  89.1 us (95%)
  local copies, waits for them, and re-layouts  2.9 us (3%)
  between operations  1.29 us (1%)
    pallas_call x1, Pallas kernels, shards(): pl.pallas_call(kernel, out_shape=(jax.ShapeDtypeStruct((128, CHUNK), BF),...  89.1 us

profile of v4, /device:TPU:1, one launch (start us, length us, event | category | flops | bytes accessed | tf_op | source)
XLA Modules:
  0.0 93.3 jit_solution(11178138549456510209)
XLA Ops:
  1.3 89.1 %shard_map.95 = (bf16[128,464]{1,0:T(8,128)(2,1)}, s32[2,58]{1,0:T(2,128)}) custom-call(s32[1]{0:T(128)S(6)} %copy.12.count_ref, s32[1,7]{1,0:T(1,128)} %drop_ref.1, s32[1,7]{1,0:T(1,128)} %grow_ref.1, s32[2,58]{1,0:T(2,128)} %old_ref.1, bf16[8,7424]{1,0:T(8,128)(2,1)} %grad_ref.1, bf16[8,32768]{1,0:T(8,128)(2,1)} %hid_ref.1, ...), custom_call_target="tpu_custom_call" | custom-call | flops 8000000000 | bytes 10000000 | tf_op jit(solution)/shard_map/pallas_call | solution.py:498
  90.4 1.7 %copy.10 = bf16[128,464]{0,1:T(8,128)(2,1)} copy(bf16[128,464]{1,0:T(8,128)(2,1)} %get-tuple-element.2) | data formatting | bytes 237568 | tf_op jit(solution)/shard_map/pallas_call | solution.py:498
  92.0 1.2 %copy.13 = s32[2,58]{1,0:T(2,128)} copy(s32[2,58]{1,0:T(2,128)} %get-tuple-element.7) | data formatting | bytes 928

commit v5 on v4

--- a/solution.py
+++ b/solution.py
@@ -26,7 +26,7 @@
 FAR = (1, 3, 2)
 TURNS = (("x", "y", "z"), ("y", "z", "x"))
 GATHER = (("x", "y", "z"), ("y", "z", "x"), ("z", "x", "y"))
-SCATTER = (("x", "y", "z"), ("y", "z", "x"), ("z", "x", "y"))
+SCATTER = (("z", "x", "y"), ("x", "y", "z"), ("y", "z", "x"))
 GDIMS = ("x", "y", "z")
 SDIMS = ("z", "x", "y")
 
@@ -154,6 +154,8 @@
             hid[u * 3 + q][0].wait()
         wait_for(t0.at[:, 0:3], a_recv.at[q])
 
+    for c in inp:
+        c.start()
     swap[0].wait_recv()
     g[me["x"], me["y"], me["z"]] = jnp.concatenate([gp[0], gp[1]], axis=0)
 
@@ -243,7 +245,6 @@
 
     lax.fori_loop(0, 64, sort_hidden, 0)
     hid_start(0)
-    start(inp)
 
     def spread(t, carry):
         o = pl.multiple_of(t * BLK, BLK)
@@ -268,8 +269,6 @@
             start(g1[k][p])
     hid_wait(0)
     hid_start(1)
-    swap[2].wait_recv()
-    lax.fori_loop(0, HALF // BLK, spread, 0)
     for p in range(3):
         gathered(0, p, 1)
         start(g2[0][p][:2])
@@ -280,6 +279,8 @@
     local[7].wait()
     wait_for(xin.at[0:3, own_tokens], a_recv.at[3])
     swap[5].start()
+    swap[2].wait_recv()
+    lax.fori_loop(0, HALF // BLK, spread, 0)
     for p in range(3):
         gathered(0, p, 2)
         start(g2[0][p][2:])

time: 94.1 us -> 91.6 us (0.973)
  Pallas kernels: 89.1 us -> 86.5 us
    pallas_call x1, Pallas kernels: 89.1 us -> 86.5 us  [shards(): pl.pallas_call(kernel, out_shape=(jax.ShapeDtypeStruct((128, CHUNK), BF),...]
where the time goes in v5:
time: 91.6 us; the launch traced here: 90.7 us
  Pallas kernels  86.5 us (94%)
  local copies, waits for them, and re-layouts  2.9 us (3%)
  between operations  1.29 us (1%)
    pallas_call x1, Pallas kernels, shards(): pl.pallas_call(kernel, out_shape=(jax.ShapeDtypeStruct((128, CHUNK), BF),...  86.5 us

profile of v5, /device:TPU:1, one launch (start us, length us, event | category | flops | bytes accessed | tf_op | source)
XLA Modules:
  0.0 90.7 jit_solution(16386547159822280455)
XLA Ops:
  1.3 86.5 %shard_map.95 = (bf16[128,464]{1,0:T(8,128)(2,1)}, s32[2,58]{1,0:T(2,128)}) custom-call(s32[1]{0:T(128)S(6)} %copy.12.count_ref, s32[1,7]{1,0:T(1,128)} %drop_ref.1, s32[1,7]{1,0:T(1,128)} %grow_ref.1, s32[2,58]{1,0:T(2,128)} %old_ref.1, bf16[8,7424]{1,0:T(8,128)(2,1)} %grad_ref.1, bf16[8,32768]{1,0:T(8,128)(2,1)} %hid_ref.1, ...), custom_call_target="tpu_custom_call" | custom-call | flops 8000000000 | bytes 10000000 | tf_op jit(solution)/shard_map/pallas_call | solution.py:499
  87.8 1.7 %copy.10 = bf16[128,464]{0,1:T(8,128)(2,1)} copy(bf16[128,464]{1,0:T(8,128)(2,1)} %get-tuple-element.2) | data formatting | bytes 237568 | tf_op jit(solution)/shard_map/pallas_call | solution.py:499
  89.5 1.2 %copy.13 = s32[2,58]{1,0:T(2,128)} copy(s32[2,58]{1,0:T(2,128)} %get-tuple-element.7) | data formatting | bytes 928

commit v6 on v5

--- a/solution.py
+++ b/solution.py
@@ -38,7 +38,7 @@
 def kernel(
     count_ref, drop_ref, grow_ref, old_ref, grad_ref, hid_ref, inp_ref, w_ref,
     out_ref, mask_ref,
-    count, drop, grow, old_v, grad, gm, gp, g, hb, t0, t1, t2, h, ht, acc, w, xin, s, m, expand, ra1, rb1, rb2, rb3, fin, stage, land,
+    count, drop, grow, old_v, grad, gm, gp, g, hb, t0, t1, t2, h, ht, acc, w, xin, s, m, expand, ra1, rb1, rb2, rb3, fin, stage,
     g_send, g_recv, s_send, s_recv, e_send, e_recv, f_send, f_recv, a_send, a_recv, loc,
 ):
     fsdp = lax.axis_index("fsdp")
@@ -448,7 +448,7 @@
             piece = pltpu.roll(piece, PAD + BLK - shift, 1)
         stage[k] = piece[:, :PAD].astype(BF)
         away = pltpu.make_async_remote_copy(
-            src_ref=stage.at[k], dst_ref=land.at[slot], send_sem=f_send.at[k],
+            src_ref=stage.at[k], dst_ref=out_ref.at[slot], send_sem=f_send.at[k],
             recv_sem=f_recv.at[slot], device_id=last_dev(k), device_id_type=MESH,
         )
 
@@ -458,7 +458,7 @@
 
         @pl.when(is_self(k))
         def _():
-            pltpu.make_async_copy(stage.at[k], land.at[slot], f_recv.at[slot]).start()
+            pltpu.make_async_copy(stage.at[k], out_ref.at[slot], f_recv.at[slot]).start()
 
         ends.append(away)
 
@@ -472,8 +472,7 @@
         for n in range(4 * k, 4 * k + 4):
             deliver(n)
     for k in range(8):
-        pltpu.make_async_copy(stage.at[k], land.at[k], f_recv.at[k]).wait()
-        out_ref[pl.ds(k * ROWS, ROWS), :] = land[k][:, :CHUNK]
+        pltpu.make_async_copy(stage.at[k], out_ref.at[k], f_recv.at[k]).wait()
 
     for k in range(8):
         @pl.when(jnp.logical_not(is_self(k)))
@@ -499,7 +498,7 @@
     out, mask = pl.pallas_call(
         kernel,
         out_shape=(
-            jax.ShapeDtypeStruct((128, CHUNK), BF),
+            jax.ShapeDtypeStruct((8, ROWS, PAD), BF),
             jax.ShapeDtypeStruct(old_mask.shape, jnp.int32),
         ),
         in_specs=[hbm] * 8,
@@ -531,7 +530,6 @@
             pltpu.VMEM((3, ROWS, HALF), BF),
             pltpu.VMEM((ROWS, HALF + BLK), F32),
             pltpu.VMEM((8, ROWS, PAD), BF),
-            pltpu.VMEM((8, ROWS, PAD), BF),
             dma((4,)), dma((24,)), dma((4,)), dma((24,)), dma((6,)), dma((6,)),
             dma((8,)), dma((8,)), dma((4,)), dma((4,)), dma((14,)),
         ],
@@ -540,7 +538,7 @@
         ),
         cost_estimate=pl.CostEstimate(flops=8 * 10**9, bytes_accessed=10**7, transcendentals=0),
     )(token_counts, drop_list, grow_list, old_mask, grad_out, hidden, inp, weight)
-    return (out, mask)
+    return (out.reshape(128, PAD)[:, :CHUNK], mask)
 
 
 def solution(mesh):

time: 91.6 us -> 91.6 us (level)
    pallas_call x1 -> x0, local copies, waits for them, and re-layouts: 1.68 us -> none  [shards(): pl.pallas_call(kernel, out_shape=(jax.ShapeDtypeStruct((128, CHUNK), BF),...]
    unnamed x1 -> x2, local copies, waits for them, and re-layouts: 1.23 us -> 2.9 us
where the time goes in v6:
time: 91.6 us; the launch traced here: 90.7 us
  Pallas kernels  86.5 us (94%)
  local copies, waits for them, and re-layouts  2.9 us (3%)
  between operations  1.29 us (1%)
    pallas_call x1, Pallas kernels, shards(): pl.pallas_call(kernel, out_shape=(jax.ShapeDtypeStruct((8, ROWS, PAD), BF...  86.5 us
    unnamed x2, local copies, waits for them, and re-layouts  2.9 us

profile of v6, /device:TPU:1, one launch (start us, length us, event | category | flops | bytes accessed | tf_op | source)
XLA Modules:
  0.0 90.7 jit_solution(14904570932677411254)
XLA Ops:
  1.3 86.5 %shard_map.95 = (bf16[8,16,512]{2,1,0:T(8,128)(2,1)}, s32[2,58]{1,0:T(2,128)}) custom-call(s32[1]{0:T(128)S(6)} %copy.13.count_ref, s32[1,7]{1,0:T(1,128)} %drop_ref.1, s32[1,7]{1,0:T(1,128)} %grow_ref.1, s32[2,58]{1,0:T(2,128)} %old_ref.1, bf16[8,7424]{1,0:T(8,128)(2,1)} %grad_ref.1, bf16[8,32768]{1,0:T(8,128)(2,1)} %hid_ref.1, ...), custom_call_target="tpu_custom_call" | custom-call | flops 8000000000 | bytes 10000000 | tf_op jit(solution)/shard_map/pallas_call | solution.py:498
  87.8 1.7 %copy.11 = bf16[128,464]{0,1:T(8,128)(2,1)} copy(bf16[128,464]{1,0:T(8,128)(2,1)} %bitcast.3) | data formatting | bytes 237568
  89.5 1.2 %copy.14 = s32[2,58]{1,0:T(2,128)} copy(s32[2,58]{1,0:T(2,128)} %get-tuple-element.9) | data formatting | bytes 928
